TPU v7x, 32 devices: a whole 2x2x4 slice. The times are simulated.
32 devices in a mesh: dp: 8 (over z, y), mp: 4 (over x, core).
Axes of the slice: x: 2, y: 2, z: 4, core: 2. Of those that a mesh axis runs over, the one named last changes fastest.
Arguments:
- patches: bfloat16 [4096, 1536], P('dp'), may hold values from -6 to 6
- cotangent: bfloat16 [4096, 1536], P('dp'), may hold values from -6 to 6
- item_lengths: int32 [4], replicated, may hold values from 1 to 1536, 3072 in all
- timesteps: int32 [5], replicated, may hold values from 0 to 999
- patch_rows: int32 [4096], P('dp'), may hold values from 0 to 63
- patch_cols: int32 [4096], P('dp'), may hold values from 0 to 63
- conditioning: bfloat16 [5, 1536], replicated, may hold values from -6 to 6
- text_states: bfloat16 [1280, 4096], P('dp', 'mp'), may hold values from -6 to 6
- gain_attn: bfloat16 [1536], P('dp'), may hold values from 0.5 to 1.5
- gain_ffn: bfloat16 [1536], P('dp'), may hold values from 0.5 to 1.5
- query_gain: bfloat16 [64], replicated, may hold values from 0.5 to 1.5
- key_gain: bfloat16 [64], replicated, may hold values from 0.5 to 1.5
- text_key_gain: bfloat16 [64], replicated, may hold values from 0.5 to 1.5
- cross_gate: bfloat16 [24], replicated, may hold values from -1.5 to 1.5
- w_query: bfloat16 [1536, 1536], P('dp', 'mp'), may hold values from -0.15625 to 0.15625
- w_key: bfloat16 [1536, 1536], P('dp', 'mp'), may hold values from -0.15625 to 0.15625
- w_value: bfloat16 [1536, 1536], P('dp', 'mp'), may hold values from -0.15625 to 0.15625
- w_out: bfloat16 [1536, 1536], P('dp', 'mp'), may hold values from -3 to 3
- w_text_key: bfloat16 [1536, 1536], P('dp', 'mp'), may hold values from -0.15625 to 0.15625
- w_text_value: bfloat16 [1536, 1536], P('dp', 'mp'), may hold values from -0.15625 to 0.15625
- w_gate: bfloat16 [1536, 4096], P('dp', 'mp'), may hold values from -0.15625 to 0.15625
- w_up: bfloat16 [1536, 4096], P('dp', 'mp'), may hold values from -0.15625 to 0.15625
- w_down: bfloat16 [1536, 4096], P('dp', 'mp'), may hold values from -0.09375 to 0.09375
- w_ada: bfloat16 [1536, 6144], P('dp', 'mp'), may hold values from -0.15625 to 0.15625
- w_text: bfloat16 [1536, 4096], P('dp', 'mp'), may hold values from -0.09375 to 0.09375
Outputs:
- mixed: bfloat16 [4096, 1536], P('dp')
- grad_patches: float32 [4096, 1536], P('dp')
- grad_conditioning: float32 [5, 1536], replicated
- grad_text: float32 [1280, 4096], P('dp', 'mp')
- grad_gain_attn: float32 [1536], P('dp')
- grad_gain_ffn: float32 [1536], P('dp')
- grad_query_gain: float32 [64], replicated
- grad_key_gain: float32 [64], replicated
- grad_text_key_gain: float32 [64], replicated
- grad_cross_gate: float32 [24], replicated
- grad_w_query: float32 [1536, 1536], P('dp', 'mp')
- grad_w_key: float32 [1536, 1536], P('dp', 'mp')
- grad_w_value: float32 [1536, 1536], P('dp', 'mp')
- grad_w_out: float32 [1536, 1536], P('dp', 'mp')
- grad_w_text_key: float32 [1536, 1536], P('dp', 'mp')
- grad_w_text_value: float32 [1536, 1536], P('dp', 'mp')
- grad_w_gate: float32 [1536, 4096], P('dp', 'mp')
- grad_w_up: float32 [1536, 4096], P('dp', 'mp')
- grad_w_down: float32 [1536, 4096], P('dp', 'mp')
- grad_w_ada: float32 [1536, 6144], P('dp', 'mp')
- grad_w_text: float32 [1536, 4096], P('dp', 'mp')
Inputs may be any that keep to these rules, and one draw needn't show every extreme that they name: `item_lengths`: lengths of the 4 items that fill, in order, the rows after the first 128 of each index of dp; they sum to 3072.
All inputs are finite; a program needn't handle non-finite values.
Results may differ from a plain program's by a relative error of at most 0.035.
Values may be sent and summed in bfloat16 or wider, within the bound.
No kernel may reach another device: no remote copies, remote signals or barrier semaphores. Data moves between devices by JAX's collectives and lax.ppermute only.
A program may use at most 320 MiB of HBM per device.

v0:
```python
import math

import jax
import jax.numpy as jnp
from jax import lax
from jax.sharding import PartitionSpec as P

TTOK = 256


HIGHEST = lax.Precision.HIGHEST
EPSILON = 1e-06
NEGATIVE = -1e30
SCORE_BASE = 1.4426950408889634
TWO_NATURAL = 0.6931471805599453
KEY_BLOCK = 1024


def contract(left, right, pairing, precision=None):
    return lax.dot_general(
        left, right, (pairing, ((), ())), precision=precision, preferred_element_type=jnp.float32
    )


def multiply(left, right):
    return contract(left, right, ((1,), (0,)))


def multiply_trans(left, right, precision=None):
    return contract(left, right, ((1,), (1,)), precision)


def trans_multiply(left, right, precision=None):
    return contract(left, right, ((0,), (0,)), precision)


def time_embed(steps, model_width):
    halfway = model_width // 2
    frequency = jnp.exp(-math.log(10000.0) * jnp.arange(halfway, dtype=jnp.float32) / halfway)
    phases = steps.astype(jnp.float32)[:, None] * frequency[None, :]
    return jnp.concatenate([jnp.cos(phases), jnp.sin(phases)], axis=1)


def rope_angles(rows_pos, cols_pos, head_dim):
    quarter = head_dim // 4
    frequency = jnp.exp(-math.log(10000.0) * jnp.arange(quarter, dtype=jnp.float32) / quarter)
    return jnp.concatenate(
        [
            rows_pos.astype(jnp.float32)[:, None] * frequency[None, :],
            cols_pos.astype(jnp.float32)[:, None] * frequency[None, :],
        ],
        axis=1,
    )


def rotate(tensor, angles):
    quarter = tensor.shape[-1] // 4
    cosine = jnp.cos(angles)[:, None, :]
    sine = jnp.sin(angles)[:, None, :]
    first = tensor[..., :quarter]
    second = tensor[..., quarter : 2 * quarter]
    third = tensor[..., 2 * quarter : 3 * quarter]
    fourth = tensor[..., 3 * quarter :]
    row_cos, col_cos = (cosine[..., :quarter], cosine[..., quarter:])
    row_sin, col_sin = (sine[..., :quarter], sine[..., quarter:])
    return jnp.concatenate(
        [
            first * row_cos - second * row_sin,
            first * row_sin + second * row_cos,
            third * col_cos - fourth * col_sin,
            third * col_sin + fourth * col_cos,
        ],
        axis=-1,
    )


def item_ids(lengths, tok_dev, n_dev):
    wide_dev = tok_dev // 4
    boundary = jnp.cumsum(lengths)
    position = jnp.arange(tok_dev * n_dev, dtype=jnp.int32)
    within = position % tok_dev
    placed = position // tok_dev * (tok_dev - wide_dev) + within - wide_dev
    counted = jnp.sum((boundary[None, :] <= placed[:, None]).astype(jnp.int32), axis=1)
    return jnp.where(within < wide_dev, lengths.shape[0], counted)


def norm_fwd(values, gain_vec):
    scaling = lax.rsqrt(jnp.mean(values * values, axis=-1, keepdims=True) + EPSILON)
    return (values * scaling * gain_vec, scaling)


def norm_back(values, scaling, gain_vec, incoming):
    weighted = incoming * gain_vec
    inner_mean = jnp.mean(weighted * values, axis=-1, keepdims=True)
    return (
        scaling * weighted - values * scaling * scaling * scaling * inner_mean,
        incoming * values * scaling,
    )


def touches(key_items, present):
    labels = jnp.arange(present.shape[0], dtype=jnp.int32)
    return jnp.any((key_items[:, None] == labels[None, :]) & present[None, :])


def block_scores(queries, key_block, query_items, key_items):
    scaling = queries.shape[-1] ** (-0.5) * SCORE_BASE
    raw_scores = jnp.einsum("qhd,khd->hqk", queries, key_block, preferred_element_type=jnp.float32)
    allowed = (query_items[:, None] == key_items[None, :])[None]
    return (jnp.where(allowed, raw_scores * scaling, NEGATIVE), allowed, scaling)


def absorb(state, queries, query_items, key_block, value_block, key_items):
    row_top, totals, summed = state
    scores, allowed, scaling = block_scores(queries, key_block, query_items, key_items)
    new_top = jnp.maximum(row_top, jnp.ceil(jnp.max(scores, axis=-1)))
    weights = jnp.where(allowed, jnp.exp2(scores - new_top[:, :, None]), 0.0)
    factor = jnp.exp2(row_top - new_top)
    totals = totals * factor + jnp.sum(weights, axis=-1)
    fresh = jnp.einsum(
        "hqk,khd->qhd",
        weights.astype(jnp.bfloat16),
        value_block,
        preferred_element_type=jnp.float32,
    )
    summed = summed * jnp.transpose(factor)[:, :, None] + fresh
    return (new_top, totals, summed)


def absorb_all(state, queries, query_items, key_rows, value_rows, key_items, present):
    key_count, row_width = key_rows.shape
    heads_local, head_dim = (queries.shape[1], queries.shape[2])
    blocksize = math.gcd(key_count, KEY_BLOCK)

    def absorb_advance(running, pieces):
        key_block, value_block, item_block = pieces

        def absorb_taken(current):
            return absorb(
                current,
                queries,
                query_items,
                key_block.reshape(blocksize, heads_local, head_dim),
                value_block.reshape(blocksize, heads_local, head_dim),
                item_block,
            )

        def absorb_passed(current):
            return current

        return (lax.cond(touches(item_block, present), absorb_taken, absorb_passed, running), None)

    running, _ = lax.scan(
        absorb_advance,
        state,
        (
            key_rows.reshape(key_count // blocksize, blocksize, row_width),
            value_rows.reshape(key_count // blocksize, blocksize, row_width),
            key_items.reshape(key_count // blocksize, blocksize),
        ),
    )
    return running


def release_all(
    queries,
    query_items,
    key_rows,
    value_rows,
    key_items,
    row_top,
    grad_summed,
    grad_totals,
    present,
):
    key_count, row_width = key_rows.shape
    heads_local, head_dim = (queries.shape[1], queries.shape[2])
    blocksize = math.gcd(key_count, KEY_BLOCK)

    def release_advance(grad_queries, pieces):
        key_block, value_block, item_block = pieces

        def release_taken(current):
            key_heads = key_block.reshape(blocksize, heads_local, head_dim)
            value_heads = value_block.reshape(blocksize, heads_local, head_dim)
            scores, allowed, scaling = block_scores(queries, key_heads, query_items, item_block)
            weights = jnp.where(allowed, jnp.exp2(scores - row_top[:, :, None]), 0.0)
            grad_weights = jnp.einsum(
                "qhd,khd->hqk", grad_summed, value_heads, preferred_element_type=jnp.float32
            )
            grad_raw = (
                weights * TWO_NATURAL * (grad_weights + grad_totals[:, :, None]) * scaling
            ).astype(jnp.bfloat16)
            updated = current + jnp.einsum(
                "hqk,khd->qhd", grad_raw, key_heads, preferred_element_type=jnp.float32
            )
            grad_keys = jnp.einsum(
                "hqk,qhd->khd", grad_raw, queries, preferred_element_type=jnp.float32
            )
            grad_values = jnp.einsum(
                "hqk,qhd->khd",
                weights.astype(jnp.bfloat16),
                grad_summed,
                preferred_element_type=jnp.float32,
            )
            return (
                updated,
                jnp.concatenate(
                    [
                        grad_keys.reshape(blocksize, row_width),
                        grad_values.reshape(blocksize, row_width),
                    ],
                    axis=1,
                ),
            )

        def release_passed(current):
            return (current, jnp.zeros((blocksize, 2 * row_width), jnp.float32))

        return lax.cond(touches(item_block, present), release_taken, release_passed, grad_queries)

    grad_queries, key_terms = lax.scan(
        release_advance,
        jnp.zeros(queries.shape, jnp.float32),
        (
            key_rows.reshape(key_count // blocksize, blocksize, row_width),
            value_rows.reshape(key_count // blocksize, blocksize, row_width),
            key_items.reshape(key_count // blocksize, blocksize),
        ),
    )
    return (grad_queries, key_terms.reshape(key_count, 2 * row_width))


def head_grads(incoming, outputs, totals):
    totals_t = jnp.transpose(totals)[:, :, None]
    grad_summed = (incoming / totals_t).astype(jnp.bfloat16)
    grad_totals = -jnp.transpose(jnp.sum(incoming * outputs, axis=-1)) / totals
    return (grad_summed, grad_totals)


def on_device(
    patches,
    cotangent,
    item_lengths,
    timesteps,
    patch_rows,
    patch_cols,
    conditioning,
    text_states,
    gain_attn,
    gain_ffn,
    query_gain,
    key_gain,
    text_key_gain,
    cross_gate,
    w_query,
    w_key,
    w_value,
    w_out,
    w_text_key,
    w_text_value,
    w_gate,
    w_up,
    w_down,
    w_ada,
    w_text,
):
    data_count = lax.axis_size("dp")
    data_index = lax.axis_index("dp")
    tok_dev, model_width = patches.shape
    head_dim = query_gain.shape[0]
    local_width = w_query.shape[1]
    heads_local = local_width // head_dim
    text_rows = text_states.shape[0]
    item_count = conditioning.shape[0]
    model_index = lax.axis_index("mp")
    gathered = (
        lax.all_gather(w_query, "dp", axis=0, tiled=True),
        lax.all_gather(w_key, "dp", axis=0, tiled=True),
        lax.all_gather(w_value, "dp", axis=0, tiled=True),
        lax.all_gather(w_out, "dp", axis=0, tiled=True),
        lax.all_gather(w_text_key, "dp", axis=0, tiled=True),
        lax.all_gather(w_text_value, "dp", axis=0, tiled=True),
        lax.all_gather(w_gate, "dp", axis=0, tiled=True),
        lax.all_gather(w_up, "dp", axis=0, tiled=True),
        lax.all_gather(w_down, "dp", axis=0, tiled=True),
        lax.all_gather(w_ada, "dp", axis=0, tiled=True),
        lax.all_gather(w_text, "dp", axis=0, tiled=True),
        lax.all_gather(gain_attn, "dp", axis=0, tiled=True),
        lax.all_gather(gain_ffn, "dp", axis=0, tiled=True),
    )
    (
        full_query,
        full_key,
        full_value,
        full_out,
        full_text_key,
        full_text_value,
        full_gate,
        full_up,
        full_down,
        full_ada,
        full_text,
        full_gain_attn,
        full_gain_ffn,
    ) = gathered
    token_items = item_ids(item_lengths, tok_dev, data_count)
    own_items = lax.dynamic_slice_in_dim(token_items, data_index * tok_dev, tok_dev)
    text_items = jnp.arange(text_rows * data_count, dtype=jnp.int32) // TTOK
    item_labels = jnp.arange(item_count, dtype=jnp.int32)
    onehot = (own_items[:, None] == item_labels[None, :]).astype(jnp.float32)
    present = jnp.any(own_items[:, None] == item_labels[None, :], axis=0)
    angles = rope_angles(patch_rows, patch_cols, head_dim)
    embed_pre = conditioning.astype(jnp.float32) + time_embed(timesteps, model_width)
    embed = jax.nn.silu(embed_pre).astype(jnp.bfloat16)
    mod_part = multiply(embed, full_ada)
    modulation = lax.all_gather(mod_part.astype(jnp.bfloat16), "mp", axis=1, tiled=True).astype(
        mod_part.dtype
    )
    mod_rows = jnp.dot(onehot, modulation, precision=HIGHEST)
    shift1, gate1, shift2, gate2 = jnp.split(mod_rows, 4, axis=1)
    tanh_one, tanh_two = (jnp.tanh(gate1), jnp.tanh(gate2))
    inputs = patches.astype(jnp.float32)
    normed1, scale1 = norm_fwd(inputs, full_gain_attn.astype(jnp.float32))
    hidden1 = (normed1 * (1.0 + shift1)).astype(jnp.bfloat16)
    query_heads = multiply(hidden1, full_query).reshape(tok_dev, heads_local, head_dim)
    key_heads = multiply(hidden1, full_key).reshape(tok_dev, heads_local, head_dim)
    value_rows = multiply(hidden1, full_value).astype(jnp.bfloat16)
    query_gain32 = query_gain.astype(jnp.float32)
    key_gain32 = key_gain.astype(jnp.float32)
    query_normed, query_scale = norm_fwd(query_heads, query_gain32)
    key_normed, key_scale = norm_fwd(key_heads, key_gain32)
    queries = rotate(query_normed, angles).astype(jnp.bfloat16)
    key_rows = rotate(key_normed, angles).astype(jnp.bfloat16).reshape(tok_dev, local_width)
    words = lax.psum(multiply_trans(text_states, full_text).astype(jnp.bfloat16), "mp")
    text_key_heads = multiply(words, full_text_key).reshape(text_rows, heads_local, head_dim)
    text_gain32 = text_key_gain.astype(jnp.float32)
    text_key_normed, text_key_scale = norm_fwd(text_key_heads, text_gain32)
    text_keys = text_key_normed.astype(jnp.bfloat16).reshape(text_rows, local_width)
    text_values = multiply(words, full_text_value).astype(jnp.bfloat16)
    all_text_keys, all_text_values = (
        lax.all_gather(text_keys, "dp", axis=0, tiled=True),
        lax.all_gather(text_values, "dp", axis=0, tiled=True),
    )
    shared_keys, shared_values = (key_rows, value_rows)
    start_state = (
        jnp.full((heads_local, tok_dev), NEGATIVE, jnp.float32),
        jnp.zeros((heads_local, tok_dev), jnp.float32),
        jnp.zeros((tok_dev, heads_local, head_dim), jnp.float32),
    )
    self_state = absorb_all(
        start_state,
        queries,
        own_items,
        lax.all_gather(shared_keys, "dp", axis=0, tiled=True),
        lax.all_gather(shared_values, "dp", axis=0, tiled=True),
        token_items,
        present,
    )
    self_top, self_totals, self_summed = self_state
    cross_top, cross_totals, cross_summed = absorb_all(
        start_state, queries, own_items, all_text_keys, all_text_values, text_items, present
    )
    self_out = self_summed / jnp.transpose(self_totals)[:, :, None]
    cross_out = cross_summed / jnp.transpose(cross_totals)[:, :, None]
    gate_local = jnp.tanh(
        lax.dynamic_slice_in_dim(
            cross_gate.astype(jnp.float32), model_index * heads_local, heads_local
        )
    )
    combined = (
        (self_out + gate_local[None, :, None] * cross_out)
        .astype(jnp.bfloat16)
        .reshape(tok_dev, local_width)
    )
    branch = lax.psum(multiply_trans(combined, full_out).astype(jnp.bfloat16), "mp").astype(
        jnp.float32
    )
    middle = inputs + tanh_one * branch
    ffn_gain32 = full_gain_ffn.astype(jnp.float32)
    normed2, scale2 = norm_fwd(middle, ffn_gain32)
    hidden2 = (normed2 * (1.0 + shift2)).astype(jnp.bfloat16)
    gate_pre = multiply(hidden2, full_gate)
    up_pre = multiply(hidden2, full_up)
    logistic = jax.nn.sigmoid(gate_pre)
    silu_gate = gate_pre * logistic
    inner_act = (silu_gate * up_pre).astype(jnp.bfloat16)
    ffn_out = lax.psum(multiply_trans(inner_act, full_down).astype(jnp.bfloat16), "mp").astype(
        jnp.float32
    )
    mixed_out = (middle + tanh_two * ffn_out).astype(jnp.bfloat16)
    regathered = (
        lax.all_gather(w_query, "dp", axis=0, tiled=True),
        lax.all_gather(w_key, "dp", axis=0, tiled=True),
        lax.all_gather(w_value, "dp", axis=0, tiled=True),
        lax.all_gather(w_out, "dp", axis=0, tiled=True),
        lax.all_gather(w_text_key, "dp", axis=0, tiled=True),
        lax.all_gather(w_text_value, "dp", axis=0, tiled=True),
        lax.all_gather(w_gate, "dp", axis=0, tiled=True),
        lax.all_gather(w_up, "dp", axis=0, tiled=True),
        lax.all_gather(w_down, "dp", axis=0, tiled=True),
        lax.all_gather(w_ada, "dp", axis=0, tiled=True),
        lax.all_gather(w_text, "dp", axis=0, tiled=True),
        lax.all_gather(gain_attn, "dp", axis=0, tiled=True),
        lax.all_gather(gain_ffn, "dp", axis=0, tiled=True),
        lax.all_gather(shared_keys, "dp", axis=0, tiled=True),
        lax.all_gather(shared_values, "dp", axis=0, tiled=True),
    )
    back_weights = regathered[:13]
    back_keys, back_values = (regathered[13], regathered[14])
    (
        back_query,
        back_key,
        back_value,
        back_out,
        back_text_key,
        back_text_value,
        back_gate,
        back_up,
        back_down,
        back_ada,
        back_text,
        back_gain_attn,
        back_gain_ffn,
    ) = back_weights
    grad_output = cotangent.astype(jnp.float32)
    grad_ffn = (grad_output * tanh_two).astype(jnp.bfloat16)
    grad_inner = multiply(grad_ffn, back_down)
    grad_gate = (grad_inner * up_pre * logistic * (1.0 + gate_pre * (1.0 - logistic))).astype(
        jnp.bfloat16
    )
    grad_up = (grad_inner * silu_gate).astype(jnp.bfloat16)
    grad_hidden2 = lax.psum(
        (multiply_trans(grad_gate, back_gate) + multiply_trans(grad_up, back_up)).astype(
            jnp.bfloat16
        ),
        "mp",
    ).astype(jnp.float32)
    grad_middle_norm, gain_ffn_term = norm_back(
        middle, scale2, back_gain_ffn.astype(jnp.float32), grad_hidden2 * (1.0 + shift2)
    )
    grad_middle = grad_output + grad_middle_norm
    grad_branch = (grad_middle * tanh_one).astype(jnp.bfloat16)
    grad_combined = multiply(grad_branch, back_out).reshape(tok_dev, heads_local, head_dim)
    grad_cross_out = grad_combined * gate_local[None, :, None]
    grad_gate_local = jnp.sum(grad_combined * cross_out, axis=(0, 2)) * (
        1.0 - gate_local * gate_local
    )
    self_grad_summed, self_grad_totals = head_grads(grad_combined, self_out, self_totals)
    cross_grad_summed, cross_grad_totals = head_grads(grad_cross_out, cross_out, cross_totals)
    self_grad_queries, shared_terms = release_all(
        queries,
        own_items,
        back_keys,
        back_values,
        token_items,
        self_top,
        self_grad_summed,
        self_grad_totals,
        present,
    )
    cross_grad_queries, text_terms = release_all(
        queries,
        own_items,
        all_text_keys,
        all_text_values,
        text_items,
        cross_top,
        cross_grad_summed,
        cross_grad_totals,
        present,
    )
    shared_back, text_key_terms = (
        lax.psum_scatter(
            shared_terms.astype(jnp.bfloat16), "dp", scatter_dimension=0, tiled=True
        ).astype(jnp.float32),
        lax.psum_scatter(
            text_terms.astype(jnp.bfloat16), "dp", scatter_dimension=0, tiled=True
        ).astype(jnp.float32),
    )
    grad_query_rot = rotate(self_grad_queries + cross_grad_queries, -angles)
    grad_query_heads, query_gain_term = norm_back(
        query_heads, query_scale, query_gain32, grad_query_rot
    )
    grad_query_pre = grad_query_heads.astype(jnp.bfloat16).reshape(tok_dev, local_width)
    grad_key_rot = rotate(
        shared_back[:, :local_width].reshape(tok_dev, heads_local, head_dim), -angles
    )
    grad_key_heads, key_gain_term = norm_back(key_heads, key_scale, key_gain32, grad_key_rot)
    grad_key_pre = grad_key_heads.astype(jnp.bfloat16).reshape(tok_dev, local_width)
    grad_values = shared_back[:, local_width:].astype(jnp.bfloat16)
    grad_text_heads, text_gain_term = norm_back(
        text_key_heads,
        text_key_scale,
        text_gain32,
        text_key_terms[:, :local_width].reshape(text_rows, heads_local, head_dim),
    )
    grad_text_key_pre = grad_text_heads.astype(jnp.bfloat16).reshape(text_rows, local_width)
    grad_text_values = text_key_terms[:, local_width:].astype(jnp.bfloat16)
    hidden1_part = (
        multiply_trans(grad_query_pre, back_query)
        + multiply_trans(grad_key_pre, back_key)
        + multiply_trans(grad_values, back_value)
    )
    words_part = multiply_trans(grad_text_key_pre, back_text_key) + multiply_trans(
        grad_text_values, back_text_value
    )
    grad_hidden1, grad_words32 = (
        lax.psum(hidden1_part.astype(jnp.bfloat16), "mp").astype(jnp.float32),
        lax.psum(words_part.astype(jnp.bfloat16), "mp").astype(jnp.float32),
    )
    grad_words = grad_words32.astype(jnp.bfloat16)
    grad_inputs_norm, gain_attn_term = norm_back(
        inputs, scale1, back_gain_attn.astype(jnp.float32), grad_hidden1 * (1.0 + shift1)
    )
    grad_patches = grad_middle + grad_inputs_norm
    grad_text = multiply(grad_words, back_text)
    grad_mod_rows = jnp.concatenate(
        [
            grad_hidden1 * normed1,
            grad_middle * branch * (1.0 - tanh_one * tanh_one),
            grad_hidden2 * normed2,
            grad_output * ffn_out * (1.0 - tanh_two * tanh_two),
        ],
        axis=1,
    )
    column_width = mod_part.shape[1]
    grad_mod_own = trans_multiply(
        onehot,
        lax.dynamic_slice_in_dim(grad_mod_rows, model_index * column_width, column_width, 1),
        HIGHEST,
    )
    grad_ada = trans_multiply(embed.astype(jnp.float32), grad_mod_own, HIGHEST)
    grad_embed_part = multiply_trans(grad_mod_own, back_ada.astype(jnp.float32), HIGHEST)
    weight_grads = (
        lax.psum_scatter(
            trans_multiply(hidden1, grad_query_pre).astype(jnp.bfloat16),
            "dp",
            scatter_dimension=0,
            tiled=True,
        ).astype(jnp.float32),
        lax.psum_scatter(
            trans_multiply(hidden1, grad_key_pre).astype(jnp.bfloat16),
            "dp",
            scatter_dimension=0,
            tiled=True,
        ).astype(jnp.float32),
        lax.psum_scatter(
            trans_multiply(hidden1, grad_values).astype(jnp.bfloat16),
            "dp",
            scatter_dimension=0,
            tiled=True,
        ).astype(jnp.float32),
        lax.psum_scatter(
            trans_multiply(grad_branch, combined).astype(jnp.bfloat16),
            "dp",
            scatter_dimension=0,
            tiled=True,
        ).astype(jnp.float32),
        lax.psum_scatter(
            trans_multiply(words, grad_text_key_pre).astype(jnp.bfloat16),
            "dp",
            scatter_dimension=0,
            tiled=True,
        ).astype(jnp.float32),
        lax.psum_scatter(
            trans_multiply(words, grad_text_values).astype(jnp.bfloat16),
            "dp",
            scatter_dimension=0,
            tiled=True,
        ).astype(jnp.float32),
        lax.psum_scatter(
            trans_multiply(hidden2, grad_gate).astype(jnp.bfloat16),
            "dp",
            scatter_dimension=0,
            tiled=True,
        ).astype(jnp.float32),
        lax.psum_scatter(
            trans_multiply(hidden2, grad_up).astype(jnp.bfloat16),
            "dp",
            scatter_dimension=0,
            tiled=True,
        ).astype(jnp.float32),
        lax.psum_scatter(
            trans_multiply(grad_ffn, inner_act).astype(jnp.bfloat16),
            "dp",
            scatter_dimension=0,
            tiled=True,
        ).astype(jnp.float32),
        lax.psum_scatter(
            grad_ada.astype(jnp.bfloat16), "dp", scatter_dimension=0, tiled=True
        ).astype(jnp.float32),
        lax.psum_scatter(
            trans_multiply(grad_words, text_states).astype(jnp.bfloat16),
            "dp",
            scatter_dimension=0,
            tiled=True,
        ).astype(jnp.float32),
        lax.psum_scatter(
            jnp.sum(gain_attn_term, axis=0).astype(jnp.bfloat16),
            "dp",
            scatter_dimension=0,
            tiled=True,
        ).astype(jnp.float32),
        lax.psum_scatter(
            jnp.sum(gain_ffn_term, axis=0).astype(jnp.bfloat16),
            "dp",
            scatter_dimension=0,
            tiled=True,
        ).astype(jnp.float32),
    )
    gate_full = lax.dynamic_update_slice_in_dim(
        jnp.zeros((cross_gate.shape[0],), jnp.float32),
        grad_gate_local,
        model_index * heads_local,
        0,
    )
    grad_embed, grad_query_gain, grad_key_gain, grad_text_key_gain, grad_cross_gate = lax.psum(
        (
            grad_embed_part,
            jnp.sum(query_gain_term, axis=(0, 1)),
            jnp.sum(key_gain_term, axis=(0, 1)),
            jnp.sum(text_gain_term, axis=(0, 1)),
            gate_full,
        ),
        ("dp", "mp"),
    )
    embed_logistic = jax.nn.sigmoid(embed_pre)
    grad_conditioning = grad_embed * embed_logistic * (1.0 + embed_pre * (1.0 - embed_logistic))
    return (
        mixed_out,
        grad_patches,
        grad_conditioning,
        grad_text,
        weight_grads[11],
        weight_grads[12],
        grad_query_gain,
        grad_key_gain,
        grad_text_key_gain,
        grad_cross_gate,
        weight_grads[0],
        weight_grads[1],
        weight_grads[2],
        weight_grads[3],
        weight_grads[4],
        weight_grads[5],
        weight_grads[6],
        weight_grads[7],
        weight_grads[8],
        weight_grads[9],
        weight_grads[10],
    )


def solution(mesh):
    in_specs = (
        P("dp", None),
        P("dp", None),
        P(),
        P(),
        P("dp"),
        P("dp"),
        P(),
        P("dp", "mp"),
        P("dp"),
        P("dp"),
        P(),
        P(),
        P(),
        P(),
        P("dp", "mp"),
        P("dp", "mp"),
        P("dp", "mp"),
        P("dp", "mp"),
        P("dp", "mp"),
        P("dp", "mp"),
        P("dp", "mp"),
        P("dp", "mp"),
        P("dp", "mp"),
        P("dp", "mp"),
        P("dp", "mp"),
    )
    out_specs = (
        P("dp", None),
        P("dp", None),
        P(),
        P("dp", "mp"),
        P("dp"),
        P("dp"),
        P(),
        P(),
        P(),
        P(),
        P("dp", "mp"),
        P("dp", "mp"),
        P("dp", "mp"),
        P("dp", "mp"),
        P("dp", "mp"),
        P("dp", "mp"),
        P("dp", "mp"),
        P("dp", "mp"),
        P("dp", "mp"),
        P("dp", "mp"),
        P("dp", "mp"),
    )
    return jax.shard_map(
        on_device, mesh=mesh, in_specs=in_specs, out_specs=out_specs, check_vma=False
    )
```

profile of v0, /device:TPU:0, one launch (start us, length us, event | category | flops | bytes accessed | tf_op | source)
XLA Modules:
  0.0 2095.0 jit_solution(11467495613946698100)
XLA Ops:
  10.7 62.7 %all-gather.26.cloned.1.call-done = bf16[1536,1024]{1,0:T(8,128)(2,1)} async-done(((bf16[192,1024]{1,0:T(8,128)(2,1)}), bf16[1536,1024]{1,0:T(8,128)(2,1)}) %all-gather.26.cloned.1.call-update) | async-done | bytes 3145744 | tf_op jit(solution)/shard_map/all_gather | solution.py:288
  102.3 52.5 %all-gather.14.cloned.1.call-done = bf16[1536,1536]{1,0:T(8,128)(2,1)} async-done(((bf16[192,1536]{1,0:T(8,128)(2,1)}), bf16[1536,1536]{1,0:T(8,128)(2,1)}) %all-gather.14.cloned.1.call-update) | async-done | bytes 4718608 | tf_op jit(solution)/shard_map/all_gather | solution.py:287
  201.0 37.0 %all-gather.16.cloned.1.call-done = bf16[1536,384]{1,0:T(8,128)(2,1)} async-done(((bf16[192,384]{1,0:T(8,128)(2,1)}), bf16[1536,384]{1,0:T(8,128)(2,1)}) %all-gather.16.cloned.1.call-update) | async-done | bytes 1179664 | tf_op jit(solution)/shard_map/all_gather | solution.py:279
  245.0 35.0 %all-gather.28.cloned.1.call-done = bf16[1536,384]{1,0:T(8,128)(2,1)} async-done(((bf16[192,384]{1,0:T(8,128)(2,1)}), bf16[1536,384]{1,0:T(8,128)(2,1)}) %all-gather.28.cloned.1.call-update) | async-done | bytes 1179664 | tf_op jit(solution)/shard_map/all_gather | solution.py:282
  280.0 34.5 %all-reduce.13.cloned.1.call-done = bf16[160,1536]{1,0:T(8,128)(2,1)} async-done(((bf16[160,1536]{1,0:T(8,128)(2,1)}), bf16[160,1536]{1,0:T(8,128)(2,1)}) %all-reduce.13.cloned.1.call-update) | async-done | bytes 491536 | tf_op jit(solution)/shard_map/psum | solution.py:335
  316.8 36.0 %all_gather.79 = bf16[1280,384]{1,0:T(8,128)(2,1)} all-gather(bf16[160,384]{1,0:T(8,128)(2,1)S(1)} %multiply_convert_fusion.5), channel_id=1, replica_groups=mesh['dp'=8,'mp'=4] {'dp'}, dimensions={0}, use_global_device_ids=true | all-gather | bytes 1105920 | tf_op jit(solution)/shard_map/all_gather | solution.py:342
  363.2 36.5 %all_gather.81 = bf16[1280,384]{1,0:T(8,128)(2,1)} all-gather(bf16[160,384]{1,0:T(8,128)(2,1)S(1)} %convolution_convert_fusion.16), channel_id=1, replica_groups=mesh['dp'=8,'mp'=4] {'dp'}, dimensions={0}, use_global_device_ids=true | all-gather | bytes 1105920 | tf_op jit(solution)/shard_map/all_gather | solution.py:343
  428.5 41.0 %all-gather.24.cloned.1.call-done = bf16[4096,384]{1,0:T(8,128)(2,1)} async-done(((bf16[512,384]{1,0:T(8,128)(2,1)}), bf16[4096,384]{1,0:T(8,128)(2,1)}) %all-gather.24.cloned.1.call-update) | async-done | bytes 3145744 | tf_op jit(solution)/shard_map/all_gather | solution.py:356
  474.2 59.7 %all-gather.18.cloned.1.call-done = bf16[4096,384]{0,1:T(8,128)(2,1)} async-done(((bf16[512,384]{0,1:T(8,128)(2,1)}), bf16[4096,384]{0,1:T(8,128)(2,1)}) %all-gather.18.cloned.1.call-update) | async-done | bytes 3145744 | tf_op jit(solution)/shard_map/all_gather | solution.py:355
  544.2 53.0 %while.58 = (s32[]{:T(128)}, f32[6,512]{1,0:T(8,128)S(1)}, f32[6,512]{1,0:T(8,128)S(1)}, f32[512,6,64]{0,2,1:T(8,128)}, s32[4,1024]{1,0:T(4,128)S(1)}, /*index=5...) while((s32[]{:T(128)}, f32[6,512]{1,0:T(8,128)S(1)}, ...), condition=%wide.region_12.13_spmd, body=%wide.region_6.12_spmd.sunk | while | flops 853443584 | bytes 53037376 | solution.py:153
  605.1 39.3 %all-reduce.15.cloned.1.call-done = bf16[512,1536]{1,0:T(8,128)(2,1)} async-done(((bf16[512,1536]{1,0:T(8,128)(2,1)}), bf16[512,1536]{1,0:T(8,128)(2,1)}) %all-reduce.15.cloned.1.call-update) | async-done | bytes 1572880 | tf_op jit(solution)/shard_map/psum | solution.py:376
  651.7 55.7 %all-gather.36.cloned.1.call-done = bf16[1536,1024]{1,0:T(8,128)(2,1)} async-done(((bf16[192,1024]{1,0:T(8,128)(2,1)}), bf16[1536,1024]{1,0:T(8,128)(2,1)}) %all-gather.36.cloned.1.call-update) | async-done | bytes 3145744 | tf_op jit(solution)/shard_map/all_gather | solution.py:285
  712.4 56.4 %all-gather.34.cloned.1.call-done = bf16[1536,1024]{1,0:T(8,128)(2,1)} async-done(((bf16[192,1024]{1,0:T(8,128)(2,1)}), bf16[1536,1024]{1,0:T(8,128)(2,1)}) %all-gather.34.cloned.1.call-update) | async-done | bytes 3145744 | tf_op jit(solution)/shard_map/all_gather | solution.py:284
  774.2 55.9 %all-gather.38.cloned.1.call-done = bf16[1536,1024]{1,0:T(8,128)(2,1)} async-done(((bf16[192,1024]{1,0:T(8,128)(2,1)}), bf16[1536,1024]{1,0:T(8,128)(2,1)}) %all-gather.38.cloned.1.call-update) | async-done | bytes 3145744 | tf_op jit(solution)/shard_map/all_gather | solution.py:286
  843.8 41.4 %all-reduce.17.cloned.1.call-done = bf16[512,1536]{1,0:T(8,128)(2,1)} async-done(((bf16[512,1536]{1,0:T(8,128)(2,1)}), bf16[512,1536]{1,0:T(8,128)(2,1)}) %all-reduce.17.cloned.1.call-update) | async-done | bytes 1572880 | tf_op jit(solution)/shard_map/psum | solution.py:433
  931.8 131.8 %while.60 = (s32[]{:T(128)}, f32[512,6,64]{0,2,1:T(8,128)S(1)}, bf16[4,1024,768]{2,1,0:T(8,128)(2,1)}, s32[4,1024]{1,0:T(4,128)S(1)}, pred[5]{0:T(512)(128)(4,1)...) while((s32[]{:T(128)}, f32[512,6,64]{0,2,1:T(8,128)S(1)}, ...), condition=%wide.region_32.33_spmd, body=%wide.region_28.32_spmd.sunk | while | flops 2067479552 | bytes 79485712 | solution.py:222
  933.2 27.4 %conditional.10 = (f32[512,6,64]{0,2,1:T(8,128)S(1)}, bf16[1,1024,768]{1,2,0:T(8,128)(2,1)S(1)}) conditional(s32[]{:T(128)} %convert_element_type.505, f32[512,6,64]{0,2,1:T(8,128)S(1)} %get-tuple-element.1403, (s32[512]{0:T(512)S(1)}, s32[1024]{0:T(1024)S(1)}, bf16[4,1024,384]{1,2,0:T(8,128)(2,1)}, s32[]{:T(128)}, ...), branch_computations={%region_30.30_spmd, %region_31.31_spmd} | conditional | flops 2067464192 | bytes 73181232 | solution.py:220
  966.3 27.3 %conditional.10 = (f32[512,6,64]{0,2,1:T(8,128)S(1)}, bf16[1,1024,768]{1,2,0:T(8,128)(2,1)S(1)}) conditional(s32[]{:T(128)} %convert_element_type.505, f32[512,6,64]{0,2,1:T(8,128)S(1)} %get-tuple-element.1403, (s32[512]{0:T(512)S(1)}, s32[1024]{0:T(1024)S(1)}, bf16[4,1024,384]{1,2,0:T(8,128)(2,1)}, s32[]{:T(128)}, ...), branch_computations={%region_30.30_spmd, %region_31.31_spmd} | conditional | flops 2067464192 | bytes 73181232 | solution.py:220
  999.3 27.2 %conditional.10 = (f32[512,6,64]{0,2,1:T(8,128)S(1)}, bf16[1,1024,768]{1,2,0:T(8,128)(2,1)S(1)}) conditional(s32[]{:T(128)} %convert_element_type.505, f32[512,6,64]{0,2,1:T(8,128)S(1)} %get-tuple-element.1403, (s32[512]{0:T(512)S(1)}, s32[1024]{0:T(1024)S(1)}, bf16[4,1024,384]{1,2,0:T(8,128)(2,1)}, s32[]{:T(128)}, ...), branch_computations={%region_30.30_spmd, %region_31.31_spmd} | conditional | flops 2067464192 | bytes 73181232 | solution.py:220
  1087.4 99.0 %reduce-scatter.14.cloned.1.call-done = bf16[512,768]{1,0:T(8,128)(2,1)} async-done(((bf16[4096,768]{1,0:T(8,128)(2,1)}), bf16[512,768]{1,0:T(8,128)(2,1)}) %reduce-scatter.14.cloned.1.call-update) | async-done | bytes 786448 | tf_op jit(solution)/shard_map/reduce_scatter | solution.py:474
  1233.6 41.4 %all-reduce.19.cloned.1.call-done = (bf16[512,1536]{1,0:T(8,128)(2,1)}, bf16[512,1536]{1,0:T(8,128)(2,1)}, bf16[160,1536]{1,0:T(8,128)(2,1)}) async-done(((bf16[512,1536]{1,0:T(8,128)(2,1)}, bf16[512,1536]{1,0:T(8,128)(2,1)}, bf16[160,1536]{1,0:T(8,128)(2,1)}), (bf16[512,1536]{1,0:T(8,128)(2,1)}, bf16[512,1536]{1,0:T(8,128)(2,1)}, bf16[160,1536]{1,0:T(8,128)(2,1)})) %all-reduce.19.cloned.1.call-update) | async-done | bytes 3637264 | tf_op jit(solution)/shard_map/psum | solution.py:388
  1296.2 46.5 %reduce-scatter.24.cloned.1.call-done = bf16[192,384]{1,0:T(8,128)(2,1)} async-done(((bf16[1536,384]{1,0:T(8,128)(2,1)}), bf16[192,384]{1,0:T(8,128)(2,1)}) %reduce-scatter.24.cloned.1.call-update) | async-done | bytes 147472 | tf_op jit(solution)/shard_map/reduce_scatter | solution.py:554
  1344.4 65.9 %reduce-scatter.18.cloned.1.call-done = bf16[192,384]{1,0:T(8,128)(2,1)} async-done(((bf16[1536,384]{1,0:T(8,128)(2,1)}), bf16[192,384]{1,0:T(8,128)(2,1)}) %reduce-scatter.18.cloned.1.call-update) | async-done | bytes 147472 | tf_op jit(solution)/shard_map/reduce_scatter | solution.py:536
  1412.5 75.1 %reduce-scatter.32.cloned.1.call-done = bf16[192,1024]{1,0:T(8,128)(2,1)} async-done(((bf16[1536,1024]{1,0:T(8,128)(2,1)}), bf16[192,1024]{1,0:T(8,128)(2,1)}) %reduce-scatter.32.cloned.1.call-update) | async-done | bytes 393232 | tf_op jit(solution)/shard_map/reduce_scatter | solution.py:578
  1489.6 75.5 %reduce-scatter.30.cloned.1.call-done = bf16[192,1024]{1,0:T(8,128)(2,1)} async-done(((bf16[1536,1024]{1,0:T(8,128)(2,1)}), bf16[192,1024]{1,0:T(8,128)(2,1)}) %reduce-scatter.30.cloned.1.call-update) | async-done | bytes 393232 | tf_op jit(solution)/shard_map/reduce_scatter | solution.py:572
  1567.1 75.2 %reduce-scatter.34.cloned.1.call-done = bf16[192,1024]{1,0:T(8,128)(2,1)} async-done(((bf16[1536,1024]{1,0:T(8,128)(2,1)}), bf16[192,1024]{1,0:T(8,128)(2,1)}) %reduce-scatter.34.cloned.1.call-update) | async-done | bytes 393232 | tf_op jit(solution)/shard_map/reduce_scatter | solution.py:584
  1644.3 65.0 %reduce-scatter.28.cloned.1.call-done = bf16[192,384]{1,0:T(8,128)(2,1)} async-done(((bf16[1536,384]{1,0:T(8,128)(2,1)}), bf16[192,384]{1,0:T(8,128)(2,1)}) %reduce-scatter.28.cloned.1.call-update) | async-done | bytes 147472 | tf_op jit(solution)/shard_map/reduce_scatter | solution.py:566
  1710.9 65.1 %reduce-scatter.26.cloned.1.call-done = bf16[192,384]{1,0:T(8,128)(2,1)} async-done(((bf16[1536,384]{1,0:T(8,128)(2,1)}), bf16[192,384]{1,0:T(8,128)(2,1)}) %reduce-scatter.26.cloned.1.call-update) | async-done | bytes 147472 | tf_op jit(solution)/shard_map/reduce_scatter | solution.py:560
  1805.5 38.7 %all-reduce.4 = (f32[5,1536]{1,0:T(8,128)}, f32[64]{0:T(128)}, f32[64]{0:T(128)}, f32[64]{0:T(128)}, f32[24]{0:T(128)}) all-reduce(f32[5,1536]{1,0:T(8,128)} %fusion.151, f32[64]{0:T(128)} %reduce_sum.234, f32[64]{0:T(128)} %reduce_sum.237, f32[64]{0:T(128)} %reduce_sum.240, ...), channel_id=1, replica_groups=mesh['dp'=8,'mp'=4] {'dp','mp'}, use_global_device_ids=true, to_apply=%region_44.45 | all-reduce | flops 7896 | bytes 63168 | tf_op jit(solution)/shard_map/psum | solution.py:618
  1858.6 50.9 %reduce-scatter.22.cloned.1.call-done = bf16[192,384]{1,0:T(8,128)(2,1)} async-done(((bf16[1536,384]{1,0:T(8,128)(2,1)}), bf16[192,384]{1,0:T(8,128)(2,1)}) %reduce-scatter.22.cloned.1.call-update) | async-done | bytes 147472 | tf_op jit(solution)/shard_map/reduce_scatter | solution.py:548
  1911.2 75.9 %reduce-scatter.38.cloned.1.call-done = bf16[192,1024]{1,0:T(8,128)(2,1)} async-done(((bf16[1536,1024]{1,0:T(8,128)(2,1)}), bf16[192,1024]{1,0:T(8,128)(2,1)}) %reduce-scatter.38.cloned.1.call-update) | async-done | bytes 393232 | tf_op jit(solution)/shard_map/reduce_scatter | solution.py:593
  1989.0 96.6 %reduce-scatter.36.cloned.1.call-done = bf16[192,1536]{1,0:T(8,128)(2,1)} async-done(((bf16[1536,1536]{1,0:T(8,128)(2,1)}), bf16[192,1536]{1,0:T(8,128)(2,1)}) %reduce-scatter.36.cloned.1.call-update) | async-done | bytes 589840 | tf_op jit(solution)/shard_map/reduce_scatter | solution.py:590
  (645 shorter events, 683.8 us)
Async XLA Ops:
  7.2 66.2 %all-gather.26.cloned.1.call-start = ((), (), s32[]{:S(2)}) async-start(), calls=%async_computation.19 | async-start | bytes 3538944 | tf_op jit(solution)/shard_map/all_gather | solution.py:288
  8.0 146.8 %all-gather.14.cloned.1.call-start = ((), (), s32[]{:S(2)}) async-start(), calls=%async_computation.13 | async-start | bytes 5308416 | tf_op jit(solution)/shard_map/all_gather | solution.py:287
  8.7 187.5 %all-gather.22.cloned.1.call-start = ((), (), s32[]{:S(2)}) async-start(), calls=%async_computation.17 | async-start | bytes 1327104 | tf_op jit(solution)/shard_map/all_gather | solution.py:280
  9.5 228.6 %all-gather.16.cloned.1.call-start = ((), (), s32[]{:S(2)}) async-start(), calls=%async_computation.14 | async-start | bytes 1327104 | tf_op jit(solution)/shard_map/all_gather | solution.py:279
  10.0 269.9 %all-gather.28.cloned.1.call-start = ((), (), s32[]{:S(2)}) async-start(), calls=%async_computation.21 | async-start | bytes 1327104 | tf_op jit(solution)/shard_map/all_gather | solution.py:282
  10.7 303.8 %all-reduce.13.cloned.1.call-start = ((), (), s32[]{:S(2)}) async-start(), calls=%async_computation.20 | async-start | bytes 983040 | tf_op jit(solution)/shard_map/psum | solution.py:335
  77.3 284.0 %all-gather.30.cloned.1.call-start = ((), (), s32[]{:S(2)}) async-start(), calls=%async_computation.22 | async-start | bytes 1327104 | tf_op jit(solution)/shard_map/all_gather | solution.py:283
  78.1 328.6 %all-gather.20.cloned.1.call-start = ((), (), s32[]{:S(2)}) async-start(), calls=%async_computation.16 | async-start | bytes 1327104 | tf_op jit(solution)/shard_map/all_gather | solution.py:278
  78.8 390.7 %all-gather.24.cloned.1.call-start = ((), (), s32[]{:S(2)}) async-start(), calls=%async_computation.18 | async-start | bytes 3538944 | tf_op jit(solution)/shard_map/all_gather | solution.py:356
  199.7 334.2 %all-gather.18.cloned.1.call-start = ((), (), s32[]{:S(2)}) async-start(), calls=%async_computation.15 | async-start | bytes 3538944 | tf_op jit(solution)/shard_map/all_gather | solution.py:355
  242.7 356.9 %all-gather.32.cloned.1.call-start = ((), (), s32[]{:S(2)}) async-start(), calls=%async_computation.23 | async-start | bytes 1327104 | tf_op jit(solution)/shard_map/all_gather | solution.py:281
  243.4 401.0 %all-reduce.15.cloned.1.call-start = ((), (), s32[]{:S(2)}) async-start(), calls=%async_computation.24 | async-start | bytes 3145728 | tf_op jit(solution)/shard_map/psum | solution.py:376
  603.1 104.2 %all-gather.36.cloned.1.call-start = ((), (), s32[]{:S(2)}) async-start(), calls=%async_computation.26 | async-start | bytes 3538944 | tf_op jit(solution)/shard_map/all_gather | solution.py:285
  603.9 164.8 %all-gather.34.cloned.1.call-start = ((), (), s32[]{:S(2)}) async-start(), calls=%async_computation.25 | async-start | bytes 3538944 | tf_op jit(solution)/shard_map/all_gather | solution.py:284
  604.5 225.6 %all-gather.38.cloned.1.call-start = ((), (), s32[]{:S(2)}) async-start(), calls=%async_computation.27 | async-start | bytes 3538944 | tf_op jit(solution)/shard_map/all_gather | solution.py:286
  605.1 280.1 %all-reduce.17.cloned.1.call-start = ((), (), s32[]{:S(2)}) async-start(), calls=%async_computation.28 | async-start | bytes 3145728 | tf_op jit(solution)/shard_map/psum | solution.py:433
  843.5 230.7 %reduce-scatter.16.cloned.1.call-start = ((), (), s32[]{:S(2)}) async-start(), calls=%async_computation.30 | async-start | bytes 2211840 | tf_op jit(solution)/shard_map/reduce_scatter | solution.py:477
  931.3 255.1 %reduce-scatter.14.cloned.1.call-start = ((), (), s32[]{:S(2)}) async-start(), calls=%async_computation.29 | async-start | bytes 7077888 | tf_op jit(solution)/shard_map/reduce_scatter | solution.py:474
  1063.7 211.3 %all-reduce.19.cloned.1.call-start = ((), (), s32[]{:S(2)}) async-start(), calls=%async_computation.42 | async-start | bytes 7274496 | tf_op jit(solution)/shard_map/psum | solution.py:388
  1198.9 143.8 %reduce-scatter.24.cloned.1.call-start = ((), (), s32[]{:S(2)}) async-start(), calls=%async_computation.34 | async-start | bytes 1327104 | tf_op jit(solution)/shard_map/reduce_scatter | solution.py:554
  1203.3 206.9 %reduce-scatter.18.cloned.1.call-start = ((), (), s32[]{:S(2)}) async-start(), calls=%async_computation.31 | async-start | bytes 1327104 | tf_op jit(solution)/shard_map/reduce_scatter | solution.py:536
  1206.6 281.0 %reduce-scatter.32.cloned.1.call-start = ((), (), s32[]{:S(2)}) async-start(), calls=%async_computation.38 | async-start | bytes 3538944 | tf_op jit(solution)/shard_map/reduce_scatter | solution.py:578
  1211.5 353.6 %reduce-scatter.30.cloned.1.call-start = ((), (), s32[]{:S(2)}) async-start(), calls=%async_computation.37 | async-start | bytes 3538944 | tf_op jit(solution)/shard_map/reduce_scatter | solution.py:572
  1216.5 425.8 %reduce-scatter.34.cloned.1.call-start = ((), (), s32[]{:S(2)}) async-start(), calls=%async_computation.39 | async-start | bytes 3538944 | tf_op jit(solution)/shard_map/reduce_scatter | solution.py:584
  1223.8 485.4 %reduce-scatter.28.cloned.1.call-start = ((), (), s32[]{:S(2)}) async-start(), calls=%async_computation.36 | async-start | bytes 1327104 | tf_op jit(solution)/shard_map/reduce_scatter | solution.py:566
  1226.6 549.4 %reduce-scatter.26.cloned.1.call-start = ((), (), s32[]{:S(2)}) async-start(), calls=%async_computation.35 | async-start | bytes 1327104 | tf_op jit(solution)/shard_map/reduce_scatter | solution.py:560
  1228.3 628.7 %reduce-scatter.20.cloned.1.call-start = ((), (), s32[]{:S(2)}) async-start(), calls=%async_computation.32 | async-start | bytes 1327104 | tf_op jit(solution)/shard_map/reduce_scatter | solution.py:542
  1230.4 679.1 %reduce-scatter.22.cloned.1.call-start = ((), (), s32[]{:S(2)}) async-start(), calls=%async_computation.33 | async-start | bytes 1327104 | tf_op jit(solution)/shard_map/reduce_scatter | solution.py:548
  1233.6 753.5 %reduce-scatter.38.cloned.1.call-start = ((), (), s32[]{:S(2)}) async-start(), calls=%async_computation.41 | async-start | bytes 3538944 | tf_op jit(solution)/shard_map/reduce_scatter | solution.py:593
  1279.0 806.6 %reduce-scatter.36.cloned.1.call-start = ((), (), s32[]{:S(2)}) async-start(), calls=%async_computation.40 | async-start | bytes 5308416 | tf_op jit(solution)/shard_map/reduce_scatter | solution.py:590
  1294.8 483.5 %copy-start.78 = (bf16[1536]{0:T(1024)(128)(2,1)S(1)}, bf16[1536]{0:T(1024)(128)(2,1)}, u32[]{:S(2)}) copy-start(bf16[1536]{0:T(1024)(128)(2,1)} %get-tuple-element.821) | copy-start | bytes 9220
  1294.8 483.5 %copy-start.79 = (bf16[1536]{0:T(1024)(128)(2,1)S(1)}, bf16[1536]{0:T(1024)(128)(2,1)}, u32[]{:S(2)}) copy-start(bf16[1536]{0:T(1024)(128)(2,1)} %get-tuple-element.951) | copy-start | bytes 9220
  (123 other events, 3273.6 us)
Sparse Core Ops, SparseCore 0:
  10.3 63.1 all-gather.25
  75.6 79.1 all-gather.13
  157.0 39.1 all-gather.21
  198.2 39.8 all-gather.15
  240.1 39.8 all-gather.27
  282.8 31.7 all-reduce.12
  316.9 44.3 all-gather.29
  363.8 42.9 all-gather.19
  409.7 59.7 all-gather.23
  472.2 61.6 all-gather.17
  536.3 39.2 all-gather.31
  603.3 41.0 all-reduce.14
  646.8 60.5 all-gather.35
  709.6 59.0 all-gather.33
  771.0 59.0 all-gather.37
  843.6 41.4 all-reduce.16
  931.4 71.3 reduce-scatter.15
  1063.8 122.5 reduce-scatter.13
  1199.0 75.9 all-reduce.18
  1278.6 64.0 reduce-scatter.23
  1347.1 63.1 reduce-scatter.17
  1414.3 73.3 reduce-scatter.31
  1491.7 73.4 reduce-scatter.29
  1569.0 73.2 reduce-scatter.33
  1646.1 63.1 reduce-scatter.27
  1712.9 63.0 reduce-scatter.25
  1779.6 63.0 reduce-scatter.19
  1846.4 63.0 reduce-scatter.21
  1913.6 73.4 reduce-scatter.37
  1991.0 94.5 reduce-scatter.35
where the time goes:
time: 2110 us; the launch traced here: 2100 us
  waiting for transfers between devices  1450 us (69%)
  matrix products  251 us (12%)
  blocking collectives  158 us (7%)
  other arithmetic  116 us (5%)
  local copies, waits for them, and re-layouts  90.1 us (4%)
    dot_general x34, matrix products, contract(): lax.dot_general(left, right, (pairing, ((), ())), precision=precision, pr...  111 us
    reduce_scatter x1, waiting for transfers between devices, on_device(): lax.psum_scatter(shared_terms.astype(jnp.bfloat16), 'dp', scatter_dimensi...  99 us
    reduce_scatter x1, waiting for transfers between devices, on_device(): lax.psum_scatter(grad_ada.astype(jnp.bfloat16), 'dp', scatter_dimension=0...  96.6 us
    reduce_scatter x1, waiting for transfers between devices, on_device(): lax.psum_scatter(trans_multiply(grad_words, text_states).astype(jnp.bfloa...  75.9 us
    reduce_scatter x1, waiting for transfers between devices, on_device(): lax.psum_scatter(trans_multiply(hidden2, grad_gate).astype(jnp.bfloat16),...  75.5 us
    reduce_scatter x1, waiting for transfers between devices, on_device(): lax.psum_scatter(trans_multiply(grad_ffn, inner_act).astype(jnp.bfloat16)...  75.2 us
    reduce_scatter x1, waiting for transfers between devices, on_device(): lax.psum_scatter(trans_multiply(hidden2, grad_up).astype(jnp.bfloat16), '...  75.1 us
    reduce_scatter x1, waiting for transfers between devices, on_device(): lax.psum_scatter(trans_multiply(hidden1, grad_query_pre).astype(jnp.bfloa...  65.9 us
  transfers between devices with their start and end apart: 30, of which 27 were waited for; matrix products, arithmetic and copies ran while one was open for 18% of the time, Pallas kernels for 0%

commit v1 on v0

v1 whole, which is shorter than its diff:
```python
import math

import jax
import jax.numpy as jnp
from jax import lax
from jax.sharding import PartitionSpec as P

TTOK = 256
HIGHEST = lax.Precision.HIGHEST
EPSILON = 1e-06
NEGATIVE = -1e30
SCORE_BASE = 1.4426950408889634
TWO_NATURAL = 0.6931471805599453
KEY_BLOCK = 1024
AXES = ("dp", "mp")
LANES = 128
F32 = jnp.float32
BF16 = jnp.bfloat16


def contract(left, right, pairing, precision=None):
    return lax.dot_general(
        left, right, (pairing, ((), ())), precision=precision, preferred_element_type=F32
    )


def multiply(left, right):
    return contract(left, right, ((1,), (0,)))


def multiply_trans(left, right, precision=None):
    return contract(left, right, ((1,), (1,)), precision)


def trans_multiply(left, right, precision=None):
    return contract(left, right, ((0,), (0,)), precision)


def time_embed(steps, model_width):
    halfway = model_width // 2
    frequency = jnp.exp(-math.log(10000.0) * jnp.arange(halfway, dtype=F32) / halfway)
    phases = steps.astype(F32)[:, None] * frequency[None, :]
    return jnp.concatenate([jnp.cos(phases), jnp.sin(phases)], axis=1)


def rope_angles(rows_pos, cols_pos, head_dim):
    quarter = head_dim // 4
    frequency = jnp.exp(-math.log(10000.0) * jnp.arange(quarter, dtype=F32) / quarter)
    return jnp.concatenate(
        [
            rows_pos.astype(F32)[:, None] * frequency[None, :],
            cols_pos.astype(F32)[:, None] * frequency[None, :],
        ],
        axis=1,
    )


def rotate(tensor, angles):
    quarter = tensor.shape[-1] // 4
    cosine = jnp.cos(angles)[:, None, :]
    sine = jnp.sin(angles)[:, None, :]
    first = tensor[..., :quarter]
    second = tensor[..., quarter : 2 * quarter]
    third = tensor[..., 2 * quarter : 3 * quarter]
    fourth = tensor[..., 3 * quarter :]
    row_cos, col_cos = (cosine[..., :quarter], cosine[..., quarter:])
    row_sin, col_sin = (sine[..., :quarter], sine[..., quarter:])
    return jnp.concatenate(
        [
            first * row_cos - second * row_sin,
            first * row_sin + second * row_cos,
            third * col_cos - fourth * col_sin,
            third * col_sin + fourth * col_cos,
        ],
        axis=-1,
    )


def item_ids(lengths, tok_dev, n_dev):
    wide_dev = tok_dev // 4
    boundary = jnp.cumsum(lengths)
    position = jnp.arange(tok_dev * n_dev, dtype=jnp.int32)
    within = position % tok_dev
    placed = position // tok_dev * (tok_dev - wide_dev) + within - wide_dev
    counted = jnp.sum((boundary[None, :] <= placed[:, None]).astype(jnp.int32), axis=1)
    return jnp.where(within < wide_dev, lengths.shape[0], counted)


def norm_fwd(values, gain_vec):
    scaling = lax.rsqrt(jnp.mean(values * values, axis=-1, keepdims=True) + EPSILON)
    return (values * scaling * gain_vec, scaling)


def norm_back(values, scaling, gain_vec, incoming):
    weighted = incoming * gain_vec
    inner_mean = jnp.mean(weighted * values, axis=-1, keepdims=True)
    return (
        scaling * weighted - values * scaling * scaling * scaling * inner_mean,
        incoming * values * scaling,
    )


def codes(index):
    data, model = divmod(index, 4)
    return (data // 4, data // 2 % 2, data % 2, model // 2, model % 2)


def place(dh, zl, dy, x, c):
    return ((dh * 2 + zl) * 2 + dy) * 4 + x * 2 + c


def move(values, where):
    count = lax.axis_size("dp") * lax.axis_size("mp")
    return lax.ppermute(values, AXES, [(i, place(*where(*codes(i)))) for i in range(count)])


def swap_roles(values):
    return move(values, lambda dh, zl, dy, x, c: (dh, c, dy, x, zl))


def other_core(values):
    return move(values, lambda dh, zl, dy, x, c: (dh, zl, dy, x, c ^ 1))


def other_y(values):
    return move(values, lambda dh, zl, dy, x, c: (dh, zl, dy ^ 1, x, c))


def other_high(values, high):
    return move(values, lambda dh, zl, dy, x, c: (dh ^ high, zl, dy, x, c))


def other_feature(values, other):
    return move(values, lambda dh, zl, dy, x, c: (dh, zl ^ (other & 1), dy, x ^ (other >> 1), c))


def pick(values, index, axis=0):
    return lax.dynamic_index_in_dim(values, index, axis, keepdims=False)


def after(values, *events):
    return lax.optimization_barrier((values, *events))[0]


class Place:
    def __init__(self):
        data, model = (lax.axis_index("dp"), lax.axis_index("mp"))
        self.data, self.model = (data, model)
        self.n_dp = lax.axis_size("dp")
        self.highs = self.n_dp // 4
        self.dh, self.zl, self.dy = (data // 4, data // 2 % 2, data % 2)
        self.x, self.c = (model // 2, model % 2)
        self.tokens = (self.dh * 2 + self.c) * 2 + self.dy
        self.features = self.x * 2 + self.zl


def unmix(parts, index):
    count = len(parts)
    ordered = []
    for spot in range(count):
        value = parts[spot]
        for other in range(1, count):
            value = jnp.where(index == other, parts[spot ^ other], value)
        ordered.append(value)
    return ordered


def gather_rows(shard, at, wait=()):
    rows, width = shard.shape
    half = rows // 2
    pair = shard.reshape(2, half, width)
    if wait:
        pair = after(pair, *wait)
    halves = (pick(pair, at.zl), pick(pair, 1 - at.zl))
    got = [
        move(
            halves[b],
            lambda dh, zl, dy, x, c, a=a, b=b: (dh ^ a, c, dy, x, zl ^ b),
        )
        for a in range(at.highs)
        for b in (0, 1)
    ]
    near = jnp.stack(got).reshape(at.highs, 2, half, width)
    beside = other_y(near)
    near_core = other_core(near)
    beside_core = other_core(beside)
    full = jnp.zeros((at.highs, 2, 2, 2, half, width), BF16)
    for block, dy, c in (
        (near, at.dy, at.c),
        (beside, 1 - at.dy, at.c),
        (near_core, at.dy, 1 - at.c),
        (beside_core, 1 - at.dy, 1 - at.c),
    ):
        for a in range(at.highs):
            for b in (0, 1):
                full = lax.dynamic_update_slice(
                    full,
                    block[a, b][None, None, None, None],
                    (at.dh ^ a, c ^ b, dy, c, 0, 0),
                )
    return (full.reshape(at.n_dp * rows, width), got)


def scatter_rows(grads, at):
    total, width = grads.shape
    half = total // at.n_dp // 2
    view = grads.astype(BF16).reshape(at.n_dp, 2, half, width)
    kept = pick(view, at.c, 1).astype(F32) + other_core(pick(view, 1 - at.c, 1)).astype(F32)
    kept = kept.reshape(at.highs, 2, 2, half, width)
    kept = pick(kept, at.dy, 2) + other_y(pick(kept, 1 - at.dy, 2).astype(BF16)).astype(F32)
    sums = [None, None]
    for a in range(at.highs):
        for b in (0, 1):
            piece = pick(pick(kept, at.dh ^ a), at.c ^ b).astype(BF16)
            got = move(
                piece, lambda dh, zl, dy, x, c, a=a, b=b: (dh ^ a, c ^ b, dy, x, zl)
            ).astype(F32)
            sums[b] = got if sums[b] is None else sums[b] + got
    return jnp.concatenate(unmix(sums, at.zl), axis=0)


def gather_tokens(block, at):
    near = [block] + [other_high(block, a) for a in range(1, at.highs)]
    near = jnp.stack(near)
    beside = other_y(near)
    return jnp.stack([near, beside, other_core(near), other_core(beside)])


def scatter_tokens(blocks, at):
    first = blocks[0].astype(F32) + other_core(blocks[2]).astype(F32)
    second = blocks[1].astype(F32) + other_core(blocks[3]).astype(F32)
    first = first + other_y(second.astype(BF16)).astype(F32)
    total = first[0]
    for a in range(1, at.highs):
        total = total + other_high(first[a].astype(BF16), a).astype(F32)
    return total


def relative_groups(at):
    return [
        ((at.dh ^ a) * 2 + (at.c ^ core)) * 2 + (at.dy ^ y)
        for core in (0, 1)
        for y in (0, 1)
        for a in range(at.highs)
    ]


def sum_quarters(part, at):
    rows, width = part.shape
    view = part.reshape(4, rows // 4, width)
    total = pick(view, at.features).astype(F32)
    for other in (1, 2, 3):
        total = total + other_feature(pick(view, at.features ^ other), other).astype(F32)
    return total


def gather_quarters(own, at):
    parts = [own] + [other_feature(own, other) for other in (1, 2, 3)]
    return jnp.concatenate(unmix(parts, at.features), axis=0)


def gather_output(own, at):
    near = [
        move(own, lambda dh, zl, dy, x, c, a=a: (dh, c, dy, x ^ a, zl)) for a in (0, 1)
    ]
    near = jnp.stack(unmix(near, at.x))
    far = other_core(near)
    first, second = (jnp.where(at.c == 0, near, far), jnp.where(at.c == 0, far, near))
    return jnp.stack([first, second], axis=1).reshape(4 * own.shape[0], own.shape[1])


def butterfly(values, at, data=True, model=True):
    bit = 1
    while data and bit < at.n_dp:
        values = values + lax.ppermute(values, "dp", [(i, i ^ bit) for i in range(at.n_dp)])
        bit *= 2
    for bit in (1, 2) if model else ():
        values = values + lax.ppermute(values, "mp", [(i, i ^ bit) for i in range(4)])
    return values


def rows_of(table, items):
    value = jnp.broadcast_to(table[0][None], (items.shape[0], table.shape[1]))
    for item in range(1, table.shape[0]):
        value = jnp.where(items[:, None] == item, table[item][None], value)
    return value


def touches(key_items, present):
    labels = jnp.arange(present.shape[0], dtype=jnp.int32)
    return jnp.any((key_items[:, None] == labels[None, :]) & present[None, :])


def block_scores(queries, key_block, query_items, key_items):
    scaling = queries.shape[-1] ** (-0.5) * SCORE_BASE
    raw_scores = jnp.einsum("qhd,khd->hqk", queries, key_block, preferred_element_type=F32)
    allowed = (query_items[:, None] == key_items[None, :])[None]
    return (jnp.where(allowed, raw_scores * scaling, NEGATIVE), allowed, scaling)


def absorb(state, queries, query_items, key_block, value_block, key_items):
    row_top, totals, summed = state
    scores, allowed, scaling = block_scores(queries, key_block, query_items, key_items)
    new_top = jnp.maximum(row_top, jnp.ceil(jnp.max(scores, axis=-1)))
    weights = jnp.where(allowed, jnp.exp2(scores - new_top[:, :, None]), 0.0)
    factor = jnp.exp2(row_top - new_top)
    totals = totals * factor + jnp.sum(weights, axis=-1)
    fresh = jnp.einsum(
        "hqk,khd->qhd",
        weights.astype(BF16),
        value_block,
        preferred_element_type=F32,
    )
    summed = summed * jnp.transpose(factor)[:, :, None] + fresh
    return (new_top, totals, summed)


def absorb_all(state, queries, query_items, key_rows, value_rows, key_items, present):
    key_count, row_width = key_rows.shape
    heads_local, head_dim = (queries.shape[1], queries.shape[2])
    blocksize = math.gcd(key_count, KEY_BLOCK)

    def absorb_advance(running, pieces):
        key_block, value_block, item_block = pieces

        def absorb_taken(current):
            return absorb(
                current,
                queries,
                query_items,
                key_block.reshape(blocksize, heads_local, head_dim),
                value_block.reshape(blocksize, heads_local, head_dim),
                item_block,
            )

        def absorb_passed(current):
            return current

        return (lax.cond(touches(item_block, present), absorb_taken, absorb_passed, running), None)

    running, _ = lax.scan(
        absorb_advance,
        state,
        (
            key_rows.reshape(key_count // blocksize, blocksize, row_width),
            value_rows.reshape(key_count // blocksize, blocksize, row_width),
            key_items.reshape(key_count // blocksize, blocksize),
        ),
    )
    return running


def release_all(
    queries,
    query_items,
    key_rows,
    value_rows,
    key_items,
    row_top,
    grad_summed,
    grad_totals,
    present,
):
    key_count, row_width = key_rows.shape
    heads_local, head_dim = (queries.shape[1], queries.shape[2])
    blocksize = math.gcd(key_count, KEY_BLOCK)

    def release_advance(grad_queries, pieces):
        key_block, value_block, item_block = pieces

        def release_taken(current):
            key_heads = key_block.reshape(blocksize, heads_local, head_dim)
            value_heads = value_block.reshape(blocksize, heads_local, head_dim)
            scores, allowed, scaling = block_scores(queries, key_heads, query_items, item_block)
            weights = jnp.where(allowed, jnp.exp2(scores - row_top[:, :, None]), 0.0)
            grad_weights = jnp.einsum(
                "qhd,khd->hqk", grad_summed, value_heads, preferred_element_type=F32
            )
            grad_raw = (
                weights * TWO_NATURAL * (grad_weights + grad_totals[:, :, None]) * scaling
            ).astype(BF16)
            updated = current + jnp.einsum(
                "hqk,khd->qhd", grad_raw, key_heads, preferred_element_type=F32
            )
            grad_keys = jnp.einsum("hqk,qhd->khd", grad_raw, queries, preferred_element_type=F32)
            grad_values = jnp.einsum(
                "hqk,qhd->khd",
                weights.astype(BF16),
                grad_summed,
                preferred_element_type=F32,
            )
            return (
                updated,
                jnp.concatenate(
                    [
                        grad_keys.reshape(blocksize, row_width),
                        grad_values.reshape(blocksize, row_width),
                    ],
                    axis=1,
                ).astype(BF16),
            )

        def release_passed(current):
            return (current, jnp.zeros((blocksize, 2 * row_width), BF16))

        return lax.cond(touches(item_block, present), release_taken, release_passed, grad_queries)

    grad_queries, key_terms = lax.scan(
        release_advance,
        jnp.zeros(queries.shape, F32),
        (
            key_rows.reshape(key_count // blocksize, blocksize, row_width),
            value_rows.reshape(key_count // blocksize, blocksize, row_width),
            key_items.reshape(key_count // blocksize, blocksize),
        ),
    )
    return (grad_queries, key_terms.reshape(key_count, 2 * row_width))


def head_grads(incoming, outputs, totals):
    totals_t = jnp.transpose(totals)[:, :, None]
    grad_summed = (incoming / totals_t).astype(BF16)
    grad_totals = -jnp.transpose(jnp.sum(incoming * outputs, axis=-1)) / totals
    return (grad_summed, grad_totals)


def interleave(arrays):
    pairs = arrays[0].shape[-1] // LANES
    return jnp.concatenate(
        [array[..., p * LANES : (p + 1) * LANES] for p in range(pairs) for array in arrays],
        axis=-1,
    )


def separate(array, kinds):
    pairs = array.shape[-1] // LANES // kinds
    return [
        jnp.concatenate(
            [
                array[..., (p * kinds + kind) * LANES : (p * kinds + kind + 1) * LANES]
                for p in range(pairs)
            ],
            axis=-1,
        )
        for kind in range(kinds)
    ]


def on_device(
    patches,
    cotangent,
    item_lengths,
    timesteps,
    patch_rows,
    patch_cols,
    conditioning,
    text_states,
    gain_attn,
    gain_ffn,
    query_gain,
    key_gain,
    text_key_gain,
    cross_gate,
    w_query,
    w_key,
    w_value,
    w_out,
    w_text_key,
    w_text_value,
    w_gate,
    w_up,
    w_down,
    w_ada,
    w_text,
):
    at = Place()
    tok_dev, model_width = patches.shape
    shard_rows = w_query.shape[0]
    head_dim = query_gain.shape[0]
    local_width = w_query.shape[1]
    heads_local = local_width // head_dim
    text_rows = text_states.shape[0]
    item_count = conditioning.shape[0]
    quarter = tok_dev // 4
    hidden_width = w_gate.shape[1]

    my_patches = swap_roles(patches)
    positions = swap_roles(jnp.stack([patch_rows, patch_cols]).astype(F32))
    my_text = swap_roles(text_states)
    embed_pre = conditioning.astype(F32) + time_embed(timesteps, model_width)
    embed = jax.nn.silu(embed_pre).astype(BF16)
    own_embed = lax.dynamic_slice_in_dim(embed, at.data * shard_rows, shard_rows, 1)
    gains = lax.dynamic_update_slice(
        jnp.zeros((2, model_width), F32),
        jnp.stack([gain_attn, gain_ffn]).astype(F32),
        (0, at.data * shard_rows),
    )
    head_sums = butterfly(
        jnp.concatenate([multiply(own_embed, w_ada), gains], axis=0), at, model=False
    )
    gain_attn32, gain_ffn32 = (head_sums[item_count], head_sums[item_count + 1])
    mod_part = head_sums[:item_count]
    shift1_t, gate1_t, shift2_t, gate2_t = unmix(
        [mod_part]
        + [
            lax.ppermute(mod_part, "mp", [(i, i ^ other) for i in range(4)])
            for other in (1, 2, 3)
        ],
        at.model,
    )

    full_qkv, sent = gather_rows(interleave([w_query, w_key, w_value]), at)
    my_cotangent = swap_roles(after(cotangent, *sent))
    full_text, sent_text = gather_rows(w_text, at, sent)
    full_tkv, sent_tkv = gather_rows(interleave([w_text_key, w_text_value]), at, sent)
    full_out, sent_out = gather_rows(w_out, at, sent_text)
    full_gu, sent_gu = gather_rows(
        jnp.concatenate([w_gate, w_up], axis=1), at, sent_tkv + sent_out
    )
    full_down, _ = gather_rows(w_down, at, sent_tkv + sent_out)

    token_items = item_ids(item_lengths, tok_dev, at.n_dp).reshape(at.n_dp, tok_dev)
    text_items = (jnp.arange(text_rows * at.n_dp, dtype=jnp.int32) // TTOK).reshape(
        at.n_dp, text_rows
    )
    groups = relative_groups(at)
    key_items = jnp.concatenate([pick(token_items, group) for group in groups])
    text_key_items = jnp.concatenate([pick(text_items, group) for group in groups])
    own_items = pick(token_items, at.tokens)
    item_labels = jnp.arange(item_count, dtype=jnp.int32)
    onehot = (own_items[:, None] == item_labels[None, :]).astype(F32)
    present = jnp.any(own_items[:, None] == item_labels[None, :], axis=0)
    few_items = lax.dynamic_slice_in_dim(own_items, at.features * quarter, quarter)
    few_onehot = lax.dynamic_slice_in_dim(onehot, at.features * quarter, quarter)

    shift1 = rows_of(shift1_t, own_items)
    inputs = my_patches.astype(F32)
    normed1, _ = norm_fwd(inputs, gain_attn32)
    hidden1 = (normed1 * (1.0 + shift1)).astype(BF16)

    angles = rope_angles(positions[0], positions[1], head_dim)
    qkv = multiply(hidden1, full_qkv)
    query_rows, key_pre_rows, value_pre = separate(qkv, 3)
    query_heads = query_rows.reshape(tok_dev, heads_local, head_dim)
    key_heads = key_pre_rows.reshape(tok_dev, heads_local, head_dim)
    query_gain32 = query_gain.astype(F32)
    key_gain32 = key_gain.astype(F32)
    text_gain32 = text_key_gain.astype(F32)
    query_normed, query_scale = norm_fwd(query_heads, query_gain32)
    key_normed, key_scale = norm_fwd(key_heads, key_gain32)
    queries = rotate(query_normed, angles).astype(BF16)
    key_rows = rotate(key_normed, angles).astype(BF16).reshape(tok_dev, local_width)
    own_kv = interleave([key_rows, value_pre.astype(BF16)])
    all_kv = gather_tokens(own_kv, at).reshape(at.n_dp * tok_dev, 2 * local_width)
    all_keys, all_values = separate(all_kv, 2)

    words = multiply_trans(my_text, full_text).astype(BF16)
    for other in (1, 2):
        words = (words.astype(F32) + other_feature(words, other).astype(F32)).astype(BF16)
    text_pre, text_value_pre = separate(multiply(words, full_tkv), 2)
    text_key_heads = text_pre.reshape(text_rows, heads_local, head_dim)
    text_key_normed, text_key_scale = norm_fwd(text_key_heads, text_gain32)
    own_text_kv = interleave(
        [
            text_key_normed.astype(BF16).reshape(text_rows, local_width),
            text_value_pre.astype(BF16),
        ]
    )
    all_text_kv = gather_tokens(own_text_kv, at).reshape(at.n_dp * text_rows, 2 * local_width)
    all_text_keys, all_text_values = separate(all_text_kv, 2)

    start_state = (
        jnp.full((heads_local, tok_dev), NEGATIVE, F32),
        jnp.zeros((heads_local, tok_dev), F32),
        jnp.zeros((tok_dev, heads_local, head_dim), F32),
    )
    self_top, self_totals, self_summed = absorb_all(
        start_state, queries, own_items, all_keys, all_values, key_items, present
    )
    cross_top, cross_totals, cross_summed = absorb_all(
        start_state, queries, own_items, all_text_keys, all_text_values, text_key_items, present
    )
    self_out = self_summed / jnp.transpose(self_totals)[:, :, None]
    cross_out = cross_summed / jnp.transpose(cross_totals)[:, :, None]
    gate_local = jnp.tanh(
        lax.dynamic_slice_in_dim(cross_gate.astype(F32), at.features * heads_local, heads_local)
    )
    combined = (
        (self_out + gate_local[None, :, None] * cross_out)
        .astype(BF16)
        .reshape(tok_dev, local_width)
    )
    few_inputs = lax.dynamic_slice_in_dim(inputs, at.features * quarter, quarter)
    few_normed1 = lax.dynamic_slice_in_dim(normed1, at.features * quarter, quarter)
    tanh_one = jnp.tanh(rows_of(gate1_t, few_items))
    tanh_two = jnp.tanh(rows_of(gate2_t, few_items))
    shift2 = rows_of(shift2_t, few_items)
    few_shift1 = rows_of(shift1_t, few_items)
    branch = sum_quarters(multiply_trans(combined, full_out).astype(BF16), at)
    middle = few_inputs + tanh_one * branch
    normed2, scale2 = norm_fwd(middle, gain_ffn32)
    hidden2 = gather_quarters((normed2 * (1.0 + shift2)).astype(BF16), at)
    gate_up = multiply(hidden2, full_gu)
    gate_pre, up_pre = (gate_up[:, :hidden_width], gate_up[:, hidden_width:])
    logistic = jax.nn.sigmoid(gate_pre)
    silu_gate = gate_pre * logistic
    inner_act = (silu_gate * up_pre).astype(BF16)

    grad_output = my_cotangent.astype(F32)
    few_output = lax.dynamic_slice_in_dim(grad_output, at.features * quarter, quarter)
    grad_ffn = (grad_output * rows_of(jnp.tanh(gate2_t), own_items)).astype(BF16)
    grad_inner = multiply(grad_ffn, full_down)
    grad_gate = (grad_inner * up_pre * logistic * (1.0 + gate_pre * (1.0 - logistic))).astype(BF16)
    grad_up = (grad_inner * silu_gate).astype(BF16)
    grad_gu = jnp.concatenate([grad_gate, grad_up], axis=1)
    grad_hidden2 = sum_quarters(multiply_trans(grad_gu, full_gu).astype(BF16), at)

    ffn_out = sum_quarters(multiply_trans(inner_act, full_down).astype(BF16), at)
    mixed_out = gather_output((middle + tanh_two * ffn_out).astype(BF16), at)

    grad_middle_norm, gain_ffn_term = norm_back(
        middle, scale2, gain_ffn32, grad_hidden2 * (1.0 + shift2)
    )
    grad_middle = few_output + grad_middle_norm
    grad_branch = gather_quarters((grad_middle * tanh_one).astype(BF16), at)
    grad_combined = multiply(grad_branch, full_out).reshape(tok_dev, heads_local, head_dim)
    grad_cross_out = grad_combined * gate_local[None, :, None]
    grad_gate_local = jnp.sum(grad_combined * cross_out, axis=(0, 2)) * (
        1.0 - gate_local * gate_local
    )
    grads_down = scatter_rows(trans_multiply(grad_ffn, inner_act), at)
    grads_gu = scatter_rows(trans_multiply(hidden2, grad_gu), at)
    grads_out = scatter_rows(trans_multiply(grad_branch, combined), at)

    self_grad_summed, self_grad_totals = head_grads(grad_combined, self_out, self_totals)
    cross_grad_summed, cross_grad_totals = head_grads(grad_cross_out, cross_out, cross_totals)
    self_grad_queries, shared_terms = release_all(
        queries,
        own_items,
        all_keys,
        all_values,
        key_items,
        self_top,
        self_grad_summed,
        self_grad_totals,
        present,
    )
    cross_grad_queries, text_terms = release_all(
        queries,
        own_items,
        all_text_keys,
        all_text_values,
        text_key_items,
        cross_top,
        cross_grad_summed,
        cross_grad_totals,
        present,
    )
    shared_back = scatter_tokens(
        shared_terms.reshape(4, at.highs, tok_dev, 2 * local_width), at
    )
    text_back = scatter_tokens(text_terms.reshape(4, at.highs, text_rows, 2 * local_width), at)
    grad_query_rot = rotate(self_grad_queries + cross_grad_queries, -angles)
    grad_query_heads, query_gain_term = norm_back(
        query_heads, query_scale, query_gain32, grad_query_rot
    )
    grad_query_pre = grad_query_heads.astype(BF16).reshape(tok_dev, local_width)
    grad_key_rot = rotate(
        shared_back[:, :local_width].reshape(tok_dev, heads_local, head_dim), -angles
    )
    grad_key_heads, key_gain_term = norm_back(key_heads, key_scale, key_gain32, grad_key_rot)
    grad_key_pre = grad_key_heads.astype(BF16).reshape(tok_dev, local_width)
    grad_values = shared_back[:, local_width:].astype(BF16)
    grad_qkv = interleave([grad_query_pre, grad_key_pre, grad_values])
    grad_text_heads, text_gain_term = norm_back(
        text_key_heads,
        text_key_scale,
        text_gain32,
        text_back[:, :local_width].reshape(text_rows, heads_local, head_dim),
    )
    grad_tkv = interleave(
        [
            grad_text_heads.astype(BF16).reshape(text_rows, local_width),
            text_back[:, local_width:].astype(BF16),
        ]
    )
    grad_hidden1 = sum_quarters(multiply_trans(grad_qkv, full_qkv).astype(BF16), at)
    grad_words = multiply_trans(grad_tkv, full_tkv).astype(BF16)
    for other in (1, 2):
        grad_words = (
            grad_words.astype(F32) + other_feature(grad_words, other).astype(F32)
        ).astype(BF16)

    few_scale1 = lax.rsqrt(jnp.mean(few_inputs * few_inputs, axis=-1, keepdims=True) + EPSILON)
    grad_inputs_norm, gain_attn_term = norm_back(
        few_inputs, few_scale1, gain_attn32, grad_hidden1 * (1.0 + few_shift1)
    )
    grad_patches = gather_output((grad_middle + grad_inputs_norm).astype(BF16), at).astype(F32)
    grad_text = swap_roles(multiply(grad_words, full_text).astype(BF16)).astype(F32)
    grads_qkv = scatter_rows(trans_multiply(hidden1, grad_qkv), at)
    grads_tkv = scatter_rows(trans_multiply(words, grad_tkv), at)
    grads_text = scatter_rows(trans_multiply(grad_words, my_text), at)

    def item_sums(rows):
        return trans_multiply(few_onehot, rows, HIGHEST)

    early = butterfly(
        jnp.concatenate(
            [
                item_sums(grad_middle * branch * (1.0 - tanh_one * tanh_one)),
                item_sums(grad_hidden2 * normed2),
                item_sums(few_output * ffn_out * (1.0 - tanh_two * tanh_two)),
                jnp.sum(gain_ffn_term, axis=0, keepdims=True),
            ],
            axis=0,
        ),
        at,
    )
    gate_full = lax.dynamic_update_slice_in_dim(
        jnp.zeros((cross_gate.shape[0],), F32),
        grad_gate_local,
        at.features * heads_local,
        0,
    )
    small = jnp.concatenate(
        [
            jnp.sum(query_gain_term, axis=(0, 1)),
            jnp.sum(key_gain_term, axis=(0, 1)),
            jnp.sum(text_gain_term, axis=(0, 1)),
            gate_full,
        ]
    )
    small = jnp.pad(small, (0, model_width - small.shape[0]))
    late = butterfly(
        jnp.concatenate(
            [
                item_sums(grad_hidden1 * few_normed1),
                jnp.sum(gain_attn_term, axis=0, keepdims=True),
                small[None],
            ],
            axis=0,
        ),
        at,
    )
    grad_modulation = jnp.stack(
        [late[:item_count]] + [early[i * item_count : (i + 1) * item_count] for i in range(3)]
    )
    grad_mod_own = pick(grad_modulation, at.model)
    small = late[item_count + 1]
    grad_ada = trans_multiply(own_embed.astype(F32), grad_mod_own, HIGHEST)
    grad_embed_part = multiply_trans(grad_mod_own, w_ada.astype(F32), HIGHEST)
    grad_embed = butterfly(
        lax.dynamic_update_slice(
            jnp.zeros((item_count, model_width), F32),
            grad_embed_part,
            (0, at.data * shard_rows),
        ),
        at,
    )
    embed_logistic = jax.nn.sigmoid(embed_pre)
    grad_conditioning = grad_embed * embed_logistic * (1.0 + embed_pre * (1.0 - embed_logistic))
    own_gain = lambda row: lax.dynamic_slice_in_dim(row, at.data * shard_rows, shard_rows)
    grad_wq, grad_wk, grad_wv = separate(grads_qkv, 3)
    grad_wtk, grad_wtv = separate(grads_tkv, 2)
    return (
        mixed_out,
        grad_patches,
        grad_conditioning,
        grad_text,
        own_gain(late[item_count]),
        own_gain(early[3 * item_count]),
        small[:head_dim],
        small[head_dim : 2 * head_dim],
        small[2 * head_dim : 3 * head_dim],
        small[3 * head_dim : 3 * head_dim + cross_gate.shape[0]],
        grad_wq,
        grad_wk,
        grad_wv,
        grads_out,
        grad_wtk,
        grad_wtv,
        grads_gu[:, :hidden_width],
        grads_gu[:, hidden_width:],
        grads_down,
        grad_ada,
        grads_text,
    )


def solution(mesh):
    rows, both, one = (P("dp", None), P("dp", "mp"), P("dp"))
    whole = P()
    in_specs = (
        (rows, rows, whole, whole, one, one, whole, both, one, one)
        + (whole,) * 4
        + (both,) * 11
    )
    out_specs = (
        (rows, rows, whole, both, one, one) + (whole,) * 4 + (both,) * 11
    )
    return jax.shard_map(
        on_device, mesh=mesh, in_specs=in_specs, out_specs=out_specs, check_vma=False
    )
```

time: 2110 us -> 1190 us (0.56)
  waiting for transfers between devices: 1450 us -> 397 us
  starting transfers between devices: 2.46 us -> 187 us
  blocking collectives: 158 us -> 0 us
  local copies, waits for them, and re-layouts: 90.1 us -> 246 us
  matrix products: 251 us -> 182 us
  other arithmetic: 116 us -> 143 us
    reduce_scatter x13 -> x0, waiting for transfers between devices: 791 us -> none  [the longest x1 99 us: on_device(): lax.psum_scatter(shared_terms.astype(jnp.bfloat16), 'dp', scatter_dimensi...]
    all_gather x13 -> x0, waiting for transfers between devices: 492 us -> none  [the longest x1 62.7 us: on_device(): lax.all_gather(w_text, 'dp', axis=0, tiled=True)]
    ppermute x0 -> x148, waiting for transfers between devices: none -> 397 us  [the longest x127 372 us: move(): lax.ppermute(values, AXES, [(i, place(*where(*codes(i)))) for i in range(...]
    ppermute x0 -> x148, starting transfers between devices: none -> 187 us  [the longest x127 167 us: move(): lax.ppermute(values, AXES, [(i, place(*where(*codes(i)))) for i in range(...]
    psum x4 -> x0, waiting for transfers between devices: 157 us -> none  [the longest x1 41.4 us: on_device(): lax.psum(multiply_trans(inner_act, full_down).astype(jnp.bfloat16), 'mp')]
    all_gather x3 -> x0, blocking collectives: 77.8 us -> none  [the longest x1 36.5 us: on_device(): lax.all_gather(text_values, 'dp', axis=0, tiled=True)]
    dynamic_update_slice x13 -> x111, local copies, waits for them, and re-layouts: 21 us -> 93.1 us  [the longest x95 81.7 us: gather_rows(): lax.dynamic_update_slice(full, block[a, b][None, None, None, None], (at.d...]
    dot_general x34 -> x25, matrix products: 111 us -> 61.6 us  [contract(): lax.dot_general(left, right, (pairing, ((), ())), precision=precision, pr...]
  transfers between devices with their start and end apart: 30 -> 148, of which waited for: 27 -> 63; matrix products, arithmetic and copies ran while one was open for 18% -> 39% of each run, Pallas kernels for 0% -> 0%
where the time goes in v1:
time: 1190 us; the launch traced here: 1170 us
  waiting for transfers between devices  397 us (33%)
  local copies, waits for them, and re-layouts  246 us (21%)
  starting transfers between devices  187 us (16%)
  matrix products  182 us (15%)
  other arithmetic  143 us (12%)
  loops' own time  13.9 us (1%)
    ppermute x127, waiting for transfers between devices, move(): lax.ppermute(values, AXES, [(i, place(*where(*codes(i)))) for i in range(...  372 us
    ppermute x127, starting transfers between devices, move(): lax.ppermute(values, AXES, [(i, place(*where(*codes(i)))) for i in range(...  167 us
    dynamic_update_slice x95, local copies, waits for them, and re-layouts, gather_rows(): lax.dynamic_update_slice(full, block[a, b][None, None, None, None], (at.d...  81.7 us
    dot_general x25, matrix products, contract(): lax.dot_general(left, right, (pairing, ((), ())), precision=precision, pr...  61.6 us
    dot_general x8, matrix products, release_taken(): jnp.einsum('hqk,qhd->khd', weights.astype(BF16), grad_summed, preferred_e...  32 us
    unnamed x442, local copies, waits for them, and re-layouts  29.6 us
    dot_general x8, matrix products, release_taken(): jnp.einsum('qhd,khd->hqk', grad_summed, value_heads, preferred_element_ty...  29.2 us
  transfers between devices with their start and end apart: 148, of which 63 were waited for; matrix products, arithmetic and copies ran while one was open for 39% of the time, Pallas kernels for 0%

profile of v1, /device:TPU:0, one launch (start us, length us, event | category | flops | bytes accessed | tf_op | source)
XLA Modules:
  0.0 1174.6 jit_solution(2661206316536860478)
XLA Ops:
  133.1 13.3 %collective-permute-start = (bf16[512,1536]{1,0:T(8,128)(2,1)}, bf16[512,1536]{1,0:T(8,128)(2,1)}, u32[]{:S(2)}, u32[]{:S(2)}) collective-permute-start(bf16[512,1536]{1,0:T(8,128)(2,1)} %param.41), channel_id=1, source_target_pairs={{0,0},{1,8},{2,2},{3,10},{4,4},{5,12},{6,6},{7,14},{8,1},{9,9},{10... | collective-permute-start | bytes 4718600 | tf_op jit(solution)/shard_map/ppermute | solution.py:114
  159.7 20.1 %collective-permute-done.33 = bf16[2,2,96,768]{3,2,1,0:T(8,128)(2,1)S(1)} collective-permute-done((bf16[2,2,96,768]{3,2,1,0:T(8,128)(2,1)S(1)}, bf16[2,2,96,768]{3,2,1,0:T(8,128)(2,1)S(1)}, u32[]{:S(2)}, u32[]{:S(2)}) %collective-permute-start.33) | collective-permute-done | bytes 589856 | tf_op jit(solution)/shard_map/ppermute | solution.py:114
  183.4 13.4 %collective-permute-start.73 = (bf16[512,1536]{1,0:T(8,128)(2,1)}, bf16[512,1536]{1,0:T(8,128)(2,1)}, u32[]{:S(2)}, u32[]{:S(2)}) collective-permute-start(bf16[512,1536]{1,0:T(8,128)(2,1)} %param.42), channel_id=1, source_target_pairs={{0,0},{1,8},{2,2},{3,10},{4,4},{5,12},{6,6},{7,14},{8,1},{9,9},{10... | collective-permute-start | bytes 4718600 | tf_op jit(solution)/shard_map/ppermute | solution.py:114
  226.8 8.9 collective-permute-done.64
  326.6 19.0 %collective-permute-done.27 = bf16[160,1536]{1,0:T(8,128)(2,1)S(1)} collective-permute-done((bf16[160,1536]{1,0:T(8,128)(2,1)S(1)}, bf16[160,1536]{1,0:T(8,128)(2,1)S(1)}, u32[]{:S(2)}, u32[]{:S(2)}) %collective-permute-start.27) | collective-permute-done | bytes 491552 | tf_op jit(solution)/shard_map/ppermute | solution.py:114
  350.6 7.5 collective-permute-done.28
  376.6 34.8 %collective-permute-done.37 = bf16[2,160,768]{2,1,0:T(8,128)(2,1)S(1)} collective-permute-done((bf16[2,160,768]{2,1,0:T(8,128)(2,1)S(1)}, bf16[2,160,768]{2,1,0:T(8,128)(2,1)S(1)}, u32[]{:S(2)}, u32[]{:S(2)}) %collective-permute-start.37) | collective-permute-done | bytes 491552 | tf_op jit(solution)/shard_map/ppermute | solution.py:114
  422.5 23.0 %while.59 = (s32[]{:T(128)}, f32[6,512]{1,0:T(8,128)S(1)}, f32[6,512]{1,0:T(8,128)S(1)}, f32[512,6,64]{0,2,1:T(8,128)}, s32[5,256]{1,0:T(8,128)S(1)}, /*index=5*...) while((s32[]{:T(128)}, f32[6,512]{1,0:T(8,128)S(1)}, ...), condition=%wide.region_20.21_spmd, body=%wide.region_14.20_spmd.sunk | while | flops 213669632 | bytes 19601720 | solution.py:341
  466.9 52.7 %while.58 = (s32[]{:T(128)}, f32[6,512]{1,0:T(8,128)S(1)}, f32[6,512]{1,0:T(8,128)S(1)}, f32[512,6,64]{0,2,1:T(8,128)S(1)}, s32[4,1024]{1,0:T(4,128)S(1)}, /*ind...) while((s32[]{:T(128)}, f32[6,512]{1,0:T(8,128)S(1)}, ...), condition=%wide.region_12.13_spmd, body=%wide.region_6.12_spmd.sunk | while | flops 853443584 | bytes 46745856 | solution.py:341
  468.4 11.7 conditional.8
  481.6 11.7 conditional.8
  494.7 11.7 conditional.8
  507.8 11.7 conditional.8
  534.6 9.2 collective-permute-done.48
  594.7 7.9 collective-permute-done.75
  636.9 7.5 collective-permute-done.77
  658.0 37.4 %while.61 = (s32[]{:T(128)}, f32[512,6,64]{0,2,1:T(8,128)S(1)}, bf16[5,256,768]{2,1,0:T(8,128)(2,1)}, s32[5,256]{1,0:T(8,128)}, pred[5]{0:T(512)(128)(4,1)S(1)},...) while((s32[]{:T(128)}, f32[512,6,64]{0,2,1:T(8,128)S(1)}, ...), condition=%wide.region_35.36_spmd, body=%wide.region_31.35_spmd.sunk | while | flops 517213952 | bytes 23440140 | solution.py:408
  698.0 90.4 %while.60 = (s32[]{:T(128)}, f32[512,6,64]{0,2,1:T(8,128)S(1)}, bf16[4,1024,768]{1,2,0:T(8,128)(2,1)}, s32[4,1024]{1,0:T(4,128)S(1)}, pred[5]{0:T(512)(128)(4,1)...) while((s32[]{:T(128)}, f32[512,6,64]{0,2,1:T(8,128)S(1)}, ...), condition=%wide.region_29.30_spmd, body=%wide.region_25.29_spmd.sunk | while | flops 2068265984 | bytes 126671648 | solution.py:408
  699.6 19.9 %conditional.10 = (f32[512,6,64]{0,2,1:T(8,128)S(1)}, bf16[1,1024,768]{1,2,0:T(8,128)(2,1)S(1)}) conditional(s32[]{:T(128)} %convert_element_type.1351, f32[512,6,64]{0,2,1:T(8,128)S(1)} %get-tuple-element.1514, (s32[512]{0:T(512)S(1)}, s32[1024]{0:T(1024)S(1)}, bf16[4,1024,384]{1,2,0:T(8,128)(2,1)}, s32[]{:T(128)}, ...), branch_computations={%region_27.27_spmd, %region_28.28_spmd} | conditional | flops 2068250624 | bytes 123512904 | solution.py:406
  722.1 19.9 %conditional.10 = (f32[512,6,64]{0,2,1:T(8,128)S(1)}, bf16[1,1024,768]{1,2,0:T(8,128)(2,1)S(1)}) conditional(s32[]{:T(128)} %convert_element_type.1351, f32[512,6,64]{0,2,1:T(8,128)S(1)} %get-tuple-element.1514, (s32[512]{0:T(512)S(1)}, s32[1024]{0:T(1024)S(1)}, bf16[4,1024,384]{1,2,0:T(8,128)(2,1)}, s32[]{:T(128)}, ...), branch_computations={%region_27.27_spmd, %region_28.28_spmd} | conditional | flops 2068250624 | bytes 123512904 | solution.py:406
  744.7 19.9 %conditional.10 = (f32[512,6,64]{0,2,1:T(8,128)S(1)}, bf16[1,1024,768]{1,2,0:T(8,128)(2,1)S(1)}) conditional(s32[]{:T(128)} %convert_element_type.1351, f32[512,6,64]{0,2,1:T(8,128)S(1)} %get-tuple-element.1514, (s32[512]{0:T(512)S(1)}, s32[1024]{0:T(1024)S(1)}, bf16[4,1024,384]{1,2,0:T(8,128)(2,1)}, s32[]{:T(128)}, ...), branch_computations={%region_27.27_spmd, %region_28.28_spmd} | conditional | flops 2068250624 | bytes 123512904 | solution.py:406
  767.2 19.9 %conditional.10 = (f32[512,6,64]{0,2,1:T(8,128)S(1)}, bf16[1,1024,768]{1,2,0:T(8,128)(2,1)S(1)}) conditional(s32[]{:T(128)} %convert_element_type.1351, f32[512,6,64]{0,2,1:T(8,128)S(1)} %get-tuple-element.1514, (s32[512]{0:T(512)S(1)}, s32[1024]{0:T(1024)S(1)}, bf16[4,1024,384]{1,2,0:T(8,128)(2,1)}, s32[]{:T(128)}, ...), branch_computations={%region_27.27_spmd, %region_28.28_spmd} | conditional | flops 2068250624 | bytes 123512904 | solution.py:406
  831.3 12.2 %collective-permute-done.119 = bf16[2,2,96,384]{3,2,1,0:T(8,128)(2,1)S(1)} collective-permute-done((bf16[2,2,96,384]{3,2,1,0:T(8,128)(2,1)S(1)}, bf16[2,2,96,384]{3,2,1,0:T(8,128)(2,1)S(1)}, u32[]{:S(2)}, u32[]{:S(2)}) %collective-permute-start.119) | collective-permute-done | bytes 294944 | tf_op jit(solution)/shard_map/ppermute | solution.py:114
  857.6 11.7 collective-permute-done.93
  888.0 10.4 collective-permute-done.109
  927.0 34.6 %collective-permute-done.125 = bf16[2,2,96,768]{3,2,1,0:T(8,128)(2,1)S(1)} collective-permute-done((bf16[2,2,96,768]{3,2,1,0:T(8,128)(2,1)S(1)}, bf16[2,2,96,768]{3,2,1,0:T(8,128)(2,1)S(1)}, u32[]{:S(2)}, u32[]{:S(2)}) %collective-permute-start.125) | collective-permute-done | bytes 589856 | tf_op jit(solution)/shard_map/ppermute | solution.py:114
  966.3 24.6 %collective-permute-done.127 = bf16[96,768]{1,0:T(8,128)(2,1)S(1)} collective-permute-done((bf16[96,768]{1,0:T(8,128)(2,1)S(1)}, bf16[96,768]{1,0:T(8,128)(2,1)S(1)}, u32[]{:S(2)}, u32[]{:S(2)}) %collective-permute-start.127) | collective-permute-done | bytes 147488 | tf_op jit(solution)/shard_map/ppermute | solution.py:114
  1001.6 8.6 collective-permute-done.83
  1062.1 10.2 collective-permute-done.133
  1072.3 7.5 collective-permute-done.135
  1142.0 7.3 collective-permute-done.113
  1155.3 13.2 %collective-permute-done.115 = bf16[96,1152]{1,0:T(8,128)(2,1)S(1)} collective-permute-done((bf16[96,1152]{1,0:T(8,128)(2,1)S(1)}, bf16[96,1152]{1,0:T(8,128)(2,1)S(1)}, u32[]{:S(2)}, u32[]{:S(2)}) %collective-permute-start.115) | collective-permute-done | bytes 221216 | tf_op jit(solution)/shard_map/ppermute | solution.py:114
  (1368 shorter events, 911.4 us)
Async XLA Ops:
  8.3 46.0 %collective-permute-start.10 = (bf16[96,1152]{1,0:T(8,128)(2,1)S(1)}, bf16[96,1152]{1,0:T(8,128)(2,1)S(1)}, u32[]{:S(2)}, u32[]{:S(2)}) collective-permute-start(bf16[96,1152]{1,0:T(8,128)(2,1)S(1)} %get-tuple-element.1044), channel_id=1, source_target_pairs={{0,17},{1,25},{2,19},{3,27},{4,21},{5,29},{6,23},{7,31},{8,16},{9,... | collective-permute-start | bytes 663560 | tf_op jit(solution)/shard_map/ppermute | solution.py:114
  11.9 42.5 %collective-permute-start.8 = (bf16[96,1152]{1,0:T(8,128)(2,1)S(1)}, bf16[96,1152]{1,0:T(8,128)(2,1)S(1)}, u32[]{:S(2)}, u32[]{:S(2)}) collective-permute-start(bf16[96,1152]{1,0:T(8,128)(2,1)S(1)} %get-tuple-element.1044), channel_id=1, source_target_pairs={{0,1},{1,9},{2,3},{3,11},{4,5},{5,13},{6,7},{7,15},{8,0},{9,8},{10... | collective-permute-start | bytes 663560 | tf_op jit(solution)/shard_map/ppermute | solution.py:114
  47.6 264.4 %collective-permute-start.26 = (bf16[160,1024]{1,0:T(8,128)(2,1)}, bf16[160,1024]{1,0:T(8,128)(2,1)}, u32[]{:S(2)}, u32[]{:S(2)}) collective-permute-start(bf16[160,1024]{1,0:T(8,128)(2,1)} %param.48), channel_id=1, source_target_pairs={{0,0},{1,8},{2,2},{3,10},{4,4},{5,12},{6,6},{7,14},{8,1},{9,9},{10... | collective-permute-start | bytes 983048 | tf_op jit(solution)/shard_map/ppermute | solution.py:114
  133.1 114.1 %collective-permute-start = (bf16[512,1536]{1,0:T(8,128)(2,1)}, bf16[512,1536]{1,0:T(8,128)(2,1)}, u32[]{:S(2)}, u32[]{:S(2)}) collective-permute-start(bf16[512,1536]{1,0:T(8,128)(2,1)} %param.41), channel_id=1, source_target_pairs={{0,0},{1,8},{2,2},{3,10},{4,4},{5,12},{6,6},{7,14},{8,1},{9,9},{10... | collective-permute-start | bytes 4718600 | tf_op jit(solution)/shard_map/ppermute | solution.py:114
  146.5 55.5 %collective-permute-start.11 = (bf16[2,2,96,1152]{3,2,1,0:T(8,128)(2,1)}, bf16[2,2,96,1152]{3,2,1,0:T(8,128)(2,1)}, u32[]{:S(2)}, u32[]{:S(2)}) collective-permute-start(bf16[2,2,96,1152]{3,2,1,0:T(8,128)(2,1)} %bitcast.53), channel_id=1, source_target_pairs={{0,4},{1,5},{2,6},{3,7},{4,0},{5,1},{6,2},{7,3},{8,12},{9,13},{10,... | collective-permute-start | bytes 2654216 | tf_op jit(solution)/shard_map/ppermute | solution.py:114
  148.1 60.9 %collective-permute-start.12 = (bf16[2,2,96,1152]{3,2,1,0:T(8,128)(2,1)}, bf16[2,2,96,1152]{3,2,1,0:T(8,128)(2,1)}, u32[]{:S(2)}, u32[]{:S(2)}) collective-permute-start(bf16[2,2,96,1152]{3,2,1,0:T(8,128)(2,1)} %bitcast.53), channel_id=1, source_target_pairs={{0,1},{1,0},{2,3},{3,2},{4,5},{5,4},{6,7},{7,6},{8,9},{9,8},{10,11... | collective-permute-start | bytes 2654216 | tf_op jit(solution)/shard_map/ppermute | solution.py:114
  183.4 73.4 %collective-permute-start.73 = (bf16[512,1536]{1,0:T(8,128)(2,1)}, bf16[512,1536]{1,0:T(8,128)(2,1)}, u32[]{:S(2)}, u32[]{:S(2)}) collective-permute-start(bf16[512,1536]{1,0:T(8,128)(2,1)} %param.42), channel_id=1, source_target_pairs={{0,0},{1,8},{2,2},{3,10},{4,4},{5,12},{6,6},{7,14},{8,1},{9,9},{10... | collective-permute-start | bytes 4718600 | tf_op jit(solution)/shard_map/ppermute | solution.py:114
  235.7 85.5 %collective-permute-start.57 = (bf16[2,2,96,2048]{3,2,1,0:T(8,128)(2,1)}, bf16[2,2,96,2048]{3,2,1,0:T(8,128)(2,1)}, u32[]{:S(2)}, u32[]{:S(2)}) collective-permute-start(bf16[2,2,96,2048]{3,2,1,0:T(8,128)(2,1)} %bitcast.203), channel_id=1, source_target_pairs={{0,4},{1,5},{2,6},{3,7},{4,0},{5,1},{6,2},{7,3},{8,12},{9,13},{10,... | collective-permute-start | bytes 4718600 | tf_op jit(solution)/shard_map/ppermute | solution.py:114
  246.6 102.2 %collective-permute-start.58 = (bf16[2,2,96,2048]{3,2,1,0:T(8,128)(2,1)}, bf16[2,2,96,2048]{3,2,1,0:T(8,128)(2,1)}, u32[]{:S(2)}, u32[]{:S(2)}) collective-permute-start(bf16[2,2,96,2048]{3,2,1,0:T(8,128)(2,1)} %bitcast.203), channel_id=1, source_target_pairs={{0,1},{1,0},{2,3},{3,2},{4,5},{5,4},{6,7},{7,6},{8,9},{9,8},{10,11... | collective-permute-start | bytes 4718600 | tf_op jit(solution)/shard_map/ppermute | solution.py:114
  256.8 49.0 %collective-permute-start.25 = (bf16[2,2,96,1024]{3,2,1,0:T(8,128)(2,1)}, bf16[2,2,96,1024]{3,2,1,0:T(8,128)(2,1)}, u32[]{:S(2)}, u32[]{:S(2)}) collective-permute-start(bf16[2,2,96,1024]{3,2,1,0:T(8,128)(2,1)} %collective-permute-done.23), channel_id=1, source_target_pairs={{0,1},{1,0},{2,3},{3,2},{4,5},{5,4},{6,7},{7,6},{8,9},{9,8},{10,11... | collective-permute-start | bytes 2359304 | tf_op jit(solution)/shard_map/ppermute | solution.py:114
  260.6 46.2 %collective-permute-start.66 = (bf16[2,2,96,1024]{3,2,1,0:T(8,128)(2,1)}, bf16[2,2,96,1024]{3,2,1,0:T(8,128)(2,1)}, u32[]{:S(2)}, u32[]{:S(2)}) collective-permute-start(bf16[2,2,96,1024]{3,2,1,0:T(8,128)(2,1)} %collective-permute-done.64), channel_id=1, source_target_pairs={{0,1},{1,0},{2,3},{3,2},{4,5},{5,4},{6,7},{7,6},{8,9},{9,8},{10,11... | collective-permute-start | bytes 2359304 | tf_op jit(solution)/shard_map/ppermute | solution.py:114
  305.8 56.6 %collective-permute-start.15 = (bf16[512,768]{1,0:T(8,128)(2,1)}, bf16[512,768]{1,0:T(8,128)(2,1)}, u32[]{:S(2)}, u32[]{:S(2)}) collective-permute-start(bf16[512,768]{1,0:T(8,128)(2,1)} %slice_dynamic-update-slice_fusion.9), channel_id=1, source_target_pairs={{0,16},{1,17},{2,18},{3,19},{4,20},{5,21},{6,22},{7,23},{8,24},{9,... | collective-permute-start | bytes 2359304 | tf_op jit(solution)/shard_map/ppermute | solution.py:114
  321.2 90.2 %collective-permute-start.59 = (bf16[2,2,96,2048]{3,2,1,0:T(8,128)(2,1)}, bf16[2,2,96,2048]{3,2,1,0:T(8,128)(2,1)}, u32[]{:S(2)}, u32[]{:S(2)}) collective-permute-start(bf16[2,2,96,2048]{3,2,1,0:T(8,128)(2,1)} %collective-permute-done.57), channel_id=1, source_target_pairs={{0,1},{1,0},{2,3},{3,2},{4,5},{5,4},{6,7},{7,6},{8,9},{9,8},{10,11... | collective-permute-start | bytes 4718600 | tf_op jit(solution)/shard_map/ppermute | solution.py:114
  366.0 48.9 %collective-permute-start.16 = (bf16[2,512,768]{2,1,0:T(8,128)(2,1)}, bf16[2,512,768]{2,1,0:T(8,128)(2,1)}, u32[]{:S(2)}, u32[]{:S(2)}) collective-permute-start(bf16[2,512,768]{2,1,0:T(8,128)(2,1)} %get-tuple-element.964), channel_id=1, source_target_pairs={{0,4},{1,5},{2,6},{3,7},{4,0},{5,1},{6,2},{7,3},{8,12},{9,13},{10,... | collective-permute-start | bytes 4718600 | tf_op jit(solution)/shard_map/ppermute | solution.py:114
  371.9 39.4 %collective-permute-start.37 = (bf16[2,160,768]{2,1,0:T(8,128)(2,1)S(1)}, bf16[2,160,768]{2,1,0:T(8,128)(2,1)S(1)}, u32[]{:S(2)}, u32[]{:S(2)}) collective-permute-start(bf16[2,160,768]{2,1,0:T(8,128)(2,1)S(1)} %get-tuple-element.1039), channel_id=1, source_target_pairs={{0,4},{1,5},{2,6},{3,7},{4,0},{5,1},{6,2},{7,3},{8,12},{9,13},{10,... | collective-permute-start | bytes 1474568 | tf_op jit(solution)/shard_map/ppermute | solution.py:114
  376.1 69.4 %collective-permute-start.17 = (bf16[2,512,768]{2,1,0:T(8,128)(2,1)}, bf16[2,512,768]{2,1,0:T(8,128)(2,1)}, u32[]{:S(2)}, u32[]{:S(2)}) collective-permute-start(bf16[2,512,768]{2,1,0:T(8,128)(2,1)} %get-tuple-element.964), channel_id=1, source_target_pairs={{0,1},{1,0},{2,3},{3,2},{4,5},{5,4},{6,7},{7,6},{8,9},{9,8},{10,11... | collective-permute-start | bytes 4718600 | tf_op jit(solution)/shard_map/ppermute | solution.py:114
  376.1 39.4 %collective-permute-start.38 = (bf16[2,160,768]{2,1,0:T(8,128)(2,1)S(1)}, bf16[2,160,768]{2,1,0:T(8,128)(2,1)S(1)}, u32[]{:S(2)}, u32[]{:S(2)}) collective-permute-start(bf16[2,160,768]{2,1,0:T(8,128)(2,1)S(1)} %get-tuple-element.1039), channel_id=1, source_target_pairs={{0,1},{1,0},{2,3},{3,2},{4,5},{5,4},{6,7},{7,6},{8,9},{9,8},{10,11... | collective-permute-start | bytes 1474568 | tf_op jit(solution)/shard_map/ppermute | solution.py:114
  626.2 199.7 %collective-permute-start.136 = (bf16[8,96,1024]{2,1,0:T(8,128)(2,1)}, bf16[8,96,1024]{2,1,0:T(8,128)(2,1)}, u32[]{:S(2)}, u32[]{:S(2)}) collective-permute-start(bf16[8,96,1024]{2,1,0:T(8,128)(2,1)} %dynamic-slice_bitcast_fusion.3), channel_id=1, source_target_pairs={{0,1},{1,0},{2,3},{3,2},{4,5},{5,4},{6,7},{7,6},{8,9},{9,8},{10,11... | collective-permute-start | bytes 4718600 | tf_op jit(solution)/shard_map/ppermute | solution.py:114
  635.8 283.8 %collective-permute-start.130 = (bf16[8,96,2048]{2,1,0:T(8,128)(2,1)}, bf16[8,96,2048]{2,1,0:T(8,128)(2,1)}, u32[]{:S(2)}, u32[]{:S(2)}) collective-permute-start(bf16[8,96,2048]{2,1,0:T(8,128)(2,1)} %dynamic-slice_bitcast_fusion), channel_id=1, source_target_pairs={{0,1},{1,0},{2,3},{3,2},{4,5},{5,4},{6,7},{7,6},{8,9},{9,8},{10,11... | collective-permute-start | bytes 9437192 | tf_op jit(solution)/shard_map/ppermute | solution.py:114
  644.4 168.0 %collective-permute-start.70 = (bf16[128,1536]{1,0:T(8,128)(2,1)}, bf16[128,1536]{1,0:T(8,128)(2,1)}, u32[]{:S(2)}, u32[]{:S(2)}) collective-permute-start(bf16[128,1536]{1,0:T(8,128)(2,1)} %add_convert_fusion.6), channel_id=1, source_target_pairs={{0,2},{1,10},{2,0},{3,8},{4,6},{5,14},{6,4},{7,12},{8,3},{9,11},{1... | collective-permute-start | bytes 1179656 | tf_op jit(solution)/shard_map/ppermute | solution.py:114
  649.6 162.8 %collective-permute-start.71 = (bf16[128,1536]{1,0:T(8,128)(2,1)}, bf16[128,1536]{1,0:T(8,128)(2,1)}, u32[]{:S(2)}, u32[]{:S(2)}) collective-permute-start(bf16[128,1536]{1,0:T(8,128)(2,1)} %add_convert_fusion.6), channel_id=1, source_target_pairs={{0,0},{1,8},{2,2},{3,10},{4,4},{5,12},{6,6},{7,14},{8,1},{9,9},{10... | collective-permute-start | bytes 1179656 | tf_op jit(solution)/shard_map/ppermute | solution.py:114
  654.1 161.9 %collective-permute-start.103 = (f32[16,1536]{1,0:T(8,128)}, f32[16,1536]{1,0:T(8,128)}, u32[]{:S(2)}, u32[]{:S(2)}) collective-permute-start(f32[16,1536]{1,0:T(8,128)} %add.1300), channel_id=1, source_target_pairs={{0,2},{1,3},{2,0},{3,1},{4,6},{5,7},{6,4},{7,5},{8,10},{9,11},{10,... | collective-permute-start | bytes 294920 | tf_op jit(solution)/shard_map/ppermute | solution.py:278
  812.5 35.2 %collective-permute-start.90 = (bf16[2,160,768]{2,1,0:T(8,128)(2,1)S(1)}, bf16[2,160,768]{2,1,0:T(8,128)(2,1)S(1)}, u32[]{:S(2)}, u32[]{:S(2)}) collective-permute-start(bf16[2,160,768]{2,1,0:T(8,128)(2,1)S(1)} %copy-done.78), channel_id=1, source_target_pairs={{0,1},{1,0},{2,3},{3,2},{4,5},{5,4},{6,7},{7,6},{8,9},{9,8},{10,11... | collective-permute-start | bytes 1474568 | tf_op jit(solution)/shard_map/ppermute | solution.py:114
  850.5 50.3 %collective-permute-start.81 = (bf16[2,512,768]{2,1,0:T(8,128)(2,1)}, bf16[2,512,768]{2,1,0:T(8,128)(2,1)}, u32[]{:S(2)}, u32[]{:S(2)}) collective-permute-start(bf16[2,512,768]{2,1,0:T(8,128)(2,1)} %bitcast.277), channel_id=1, source_target_pairs={{0,1},{1,0},{2,3},{3,2},{4,5},{5,4},{6,7},{7,6},{8,9},{9,8},{10,11... | collective-permute-start | bytes 4718600 | tf_op jit(solution)/shard_map/ppermute | solution.py:114
  903.7 58.5 %collective-permute-start.80 = (bf16[2,512,768]{2,1,0:T(8,128)(2,1)S(1)}, bf16[2,512,768]{2,1,0:T(8,128)(2,1)S(1)}, u32[]{:S(2)}, u32[]{:S(2)}) collective-permute-start(bf16[2,512,768]{2,1,0:T(8,128)(2,1)S(1)} %bitcast.1108), channel_id=1, source_target_pairs={{0,1},{1,0},{2,3},{3,2},{4,5},{5,4},{6,7},{7,6},{8,9},{9,8},{10,11... | collective-permute-start | bytes 4718600 | tf_op jit(solution)/shard_map/ppermute | solution.py:114
  911.6 50.6 %collective-permute-start.82 = (bf16[2,512,768]{2,1,0:T(8,128)(2,1)S(1)}, bf16[2,512,768]{2,1,0:T(8,128)(2,1)S(1)}, u32[]{:S(2)}, u32[]{:S(2)}) collective-permute-start(bf16[2,512,768]{2,1,0:T(8,128)(2,1)S(1)} %add_convert_fusion), channel_id=1, source_target_pairs={{0,4},{1,5},{2,6},{3,7},{4,0},{5,1},{6,2},{7,3},{8,12},{9,13},{10,... | collective-permute-start | bytes 4718600 | tf_op jit(solution)/shard_map/ppermute | solution.py:114
  915.9 78.1 %collective-permute-start.142 = (bf16[8,96,1024]{2,1,0:T(8,128)(2,1)S(1)}, bf16[8,96,1024]{2,1,0:T(8,128)(2,1)S(1)}, u32[]{:S(2)}, u32[]{:S(2)}) collective-permute-start(bf16[8,96,1024]{2,1,0:T(8,128)(2,1)S(1)} %dynamic-slice_bitcast_fusion.2), channel_id=1, source_target_pairs={{0,1},{1,0},{2,3},{3,2},{4,5},{5,4},{6,7},{7,6},{8,9},{9,8},{10,11... | collective-permute-start | bytes 4718600 | tf_op jit(solution)/shard_map/ppermute | solution.py:114
  919.5 42.1 %collective-permute-start.125 = (bf16[2,2,96,768]{3,2,1,0:T(8,128)(2,1)S(1)}, bf16[2,2,96,768]{3,2,1,0:T(8,128)(2,1)S(1)}, u32[]{:S(2)}, u32[]{:S(2)}) collective-permute-start(bf16[2,2,96,768]{3,2,1,0:T(8,128)(2,1)S(1)} %fusion.130), channel_id=1, source_target_pairs={{0,4},{1,5},{2,6},{3,7},{4,0},{5,1},{6,2},{7,3},{8,12},{9,13},{10,... | collective-permute-start | bytes 1769480 | tf_op jit(solution)/shard_map/ppermute | solution.py:114
  924.5 74.2 %collective-permute-start.131 = (bf16[2,2,96,2048]{3,2,1,0:T(8,128)(2,1)S(1)}, bf16[2,2,96,2048]{3,2,1,0:T(8,128)(2,1)S(1)}, u32[]{:S(2)}, u32[]{:S(2)}) collective-permute-start(bf16[2,2,96,2048]{3,2,1,0:T(8,128)(2,1)S(1)} %fusion.80), channel_id=1, source_target_pairs={{0,4},{1,5},{2,6},{3,7},{4,0},{5,1},{6,2},{7,3},{8,12},{9,13},{10,... | collective-permute-start | bytes 4718600 | tf_op jit(solution)/shard_map/ppermute | solution.py:114
  997.4 116.3 %collective-permute-start.143 = (bf16[2,2,96,1024]{3,2,1,0:T(8,128)(2,1)}, bf16[2,2,96,1024]{3,2,1,0:T(8,128)(2,1)}, u32[]{:S(2)}, u32[]{:S(2)}) collective-permute-start(bf16[2,2,96,1024]{3,2,1,0:T(8,128)(2,1)} %fusion.94), channel_id=1, source_target_pairs={{0,4},{1,5},{2,6},{3,7},{4,0},{5,1},{6,2},{7,3},{8,12},{9,13},{10,... | collective-permute-start | bytes 2359304 | tf_op jit(solution)/shard_map/ppermute | solution.py:114
  1000.4 59.6 %collective-permute-start.132 = (bf16[96,2048]{1,0:T(8,128)(2,1)}, bf16[96,2048]{1,0:T(8,128)(2,1)}, u32[]{:S(2)}, u32[]{:S(2)}) collective-permute-start(bf16[96,2048]{1,0:T(8,128)(2,1)} %get-tuple-element.938), channel_id=1, source_target_pairs={{0,8},{1,0},{2,10},{3,2},{4,12},{5,4},{6,14},{7,6},{8,9},{9,1},{10... | collective-permute-start | bytes 1179656 | tf_op jit(solution)/shard_map/ppermute | solution.py:114
  1060.0 65.1 %collective-permute-start.112 = (bf16[8,96,1152]{2,1,0:T(8,128)(2,1)}, bf16[8,96,1152]{2,1,0:T(8,128)(2,1)S(1)}, u32[]{:S(2)}, u32[]{:S(2)}) collective-permute-start(bf16[8,96,1152]{2,1,0:T(8,128)(2,1)} %dynamic-slice_bitcast_fusion.1), channel_id=1, source_target_pairs={{0,1},{1,0},{2,3},{3,2},{4,5},{5,4},{6,7},{7,6},{8,9},{9,8},{10,11... | collective-permute-start | bytes 5308424 | tf_op jit(solution)/shard_map/ppermute | solution.py:114
  (334 other events, 5824.2 us)
